TPU v7x, 256 devices: a whole 4x4x8 slice. The times are simulated.
256 devices in a mesh: grp: 8 (over x_hi, y), freq: 32 (over x_lo, z, core).
Axes of the slice: x: 4 (x_hi: 2, x_lo: 2; x = x_hi * 2 + x_lo), y: 4, z: 8, core: 2. Of those that a mesh axis runs over, the one named last changes fastest.
Arguments:
- transfer: bfloat16 [512, 2, 1024, 512], P('freq', None, 'grp'), may hold values from -0.1875 to 0.1875
- adjoint: bfloat16 [512, 2, 512, 128], P('freq'), may hold values from -6 to 6
- lower_rows: bfloat16 [1048576, 384], P(('grp', 'freq')), may hold values from -6 to 6
- pivot_store: bfloat16 [1024, 384], P('grp'), may hold values from -0.3125 to 0.3125
- owners: int32 [3], replicated, may hold values from 0 to 7
- inverse_factor: bfloat16 [128, 128], replicated, as said below
Outputs:
- panel: bfloat16 [1048576, 128], P(('grp', 'freq'))
Inputs may be any that keep to these rules, and one draw needn't show every extreme that they name: `inverse_factor`: upper triangular, with diagonal entries from 0.5 to 2.
All inputs are finite; a program needn't handle non-finite values.
Results may differ from a plain program's by a relative error of at most 0.0059.
Values may be sent and summed in bfloat16 or wider, within the bound.
No kernel may reach another device: no remote copies, remote signals or barrier semaphores. Data moves between devices by JAX's collectives and lax.ppermute only.
A program may use at most 64 MiB of HBM per device.

v0:
```python
import math

import jax
import jax.numpy as jnp
from jax import lax
from jax.sharding import PartitionSpec as P

C = 128
NF = 512
PANELS = 3
NT = 1024


def broadcast(value, axis, root):
    mine = lax.axis_index(axis) == root
    return lax.psum(jnp.where(mine, value, jnp.zeros_like(value)), axis)


def make_table(samples, frequencies):
    time_steps = jnp.arange(samples, dtype=jnp.int32)[:, None]
    wave_numbers = jnp.arange(frequencies, dtype=jnp.int32)[None, :]
    phases = (time_steps * wave_numbers % samples).astype(jnp.float32) * (2.0 * math.pi / samples)
    factor = 1.0 / math.sqrt(frequencies)
    return jnp.stack([jnp.cos(phases) * factor, -jnp.sin(phases) * factor]).astype(jnp.bfloat16)


def product(left, right):
    return jnp.einsum("ksm,kmc->ksc", left, right, preferred_element_type=jnp.float32)


def per_device(transfer, adjoint, lower_rows, pivot_store, owners, inverse_factor):
    trans_real = transfer[:, 0]
    trans_imag = transfer[:, 1]
    adjoint_real = adjoint[:, 0]
    adjoint_imag = adjoint[:, 1]
    real_part = product(trans_real, adjoint_real) - product(trans_imag, adjoint_imag)
    imag_part = product(trans_real, adjoint_imag) + product(trans_imag, adjoint_real)
    spectra = jnp.stack([real_part, imag_part], axis=2).astype(jnp.bfloat16)
    table = make_table(NT, NF)
    hessian = jnp.einsum(
        "qtk,ksqc->stc",
        table,
        lax.all_to_all(spectra, "freq", split_axis=1, concat_axis=0, tiled=True),
        preferred_element_type=jnp.float32,
    )
    hessian = hessian.reshape(-1, hessian.shape[-1])
    blocks = []
    for panel_index in range(PANELS):
        own_block = pivot_store[:, panel_index * C : (panel_index + 1) * C]
        blocks.append(broadcast(own_block, "grp", owners[panel_index]))
    pivots = jnp.concatenate(blocks, axis=1)
    update = lax.dot_general(
        lower_rows, pivots, (((1,), (1,)), ((), ())), preferred_element_type=jnp.float32
    )
    reduced = (hessian - update).astype(jnp.bfloat16)
    return jnp.dot(reduced, inverse_factor, preferred_element_type=jnp.float32).astype(jnp.bfloat16)


def solution(mesh):
    in_specs = (
        P("freq", None, "grp", None),
        P("freq", None, None, None),
        P(("grp", "freq"), None),
        P("grp", None),
        P(),
        P(),
    )
    out_specs = P(("grp", "freq"), None)
    return jax.shard_map(
        per_device, mesh=mesh, in_specs=in_specs, out_specs=out_specs, check_vma=False
    )
```

profile of v0, /device:TPU:32, one launch (start us, length us, event | category | flops | bytes accessed | tf_op | source)
XLA Modules:
  0.0 127.3 jit_solution(1430206132659129587)
XLA Ops:
  6.5 3.1 %fusion.8 = f32[16,128,128]{2,1,0:T(8,128)S(1)} fusion(bf16[16,2,512,128]{3,2,1,0:T(8,128)(2,1)} %param.7, bf16[16,2,128,512]{3,2,1,0:T(8,128)(2,1)} %param.6), kind=kOutput, calls=%fused_computation.14 | convolution fusion | flops 268435456 | bytes 5242880 | tf_op jit(solution)/shard_map/ksm,kmc->ksc/dot_general | solution.py:28
  9.6 0.5 copy-done.6
  10.1 2.5 %fusion.10 = f32[16,128,128]{2,1,0:T(8,128)S(1)} fusion(bf16[16,2,512,128]{3,2,1,0:T(8,128)(2,1)S(1)} %copy-done.6, bf16[16,2,128,512]{3,2,1,0:T(8,128)(2,1)} %param.6), kind=kOutput, calls=%fused_computation.16 | convolution fusion | flops 268435456 | bytes 5242880 | tf_op jit(solution)/shard_map/ksm,kmc->ksc/dot_general | solution.py:28
  12.6 0.3 copy-done.7
  13.0 0.7 fusion.57
  13.7 0.7 fusion.52
  14.4 0.1 pad_maximum_fusion
  14.5 0.0 copy-start.5
  14.5 0.0 copy-start.3
  14.5 1.6 %copy.31 = bf16[16,128,2,128]{3,0,2,1:T(8,128)(2,1)} copy(bf16[16,128,2,128]{3,1,0,2:T(8,128)(2,1)S(1)} %pad_maximum_fusion) | data formatting | bytes 2097152 | tf_op jit(solution)/shard_map/stack | solution.py:38
  16.1 9.7 %all-to-all-start = ((bf16[16,128,2,128]{3,0,2,1:T(8,128)(2,1)}), bf16[16,128,2,128]{3,0,2,1:T(8,128)(2,1)}, u32[]{:S(2)}, u32[]{:S(2)}) async-start(bf16[16,128,2,128]{3,0,2,1:T(8,128)(2,1)} %copy.31), calls=%async_computation | async-start | bytes 2097152 | tf_op jit(solution)/shard_map/all_to_all | solution.py:43
  25.9 0.0 all-reduce.3.cloned.1.call-start
  25.9 0.7 fusion.75
  28.5 0.6 slice_select_fusion.2
  29.2 0.0 all-reduce.3.cloned.1.call-update
  29.2 9.3 %multiply_convert_fusion = (bf16[1,1024,512]{2,1,0:T(8,128)(2,1)}, bf16[1,1024,512]{2,1,0:T(8,128)(2,1)}) fusion(), kind=kLoop, calls=%fused_computation.26 | loop fusion | flops 9961472 | bytes 2097152 | tf_op jit(solution)/shard_map/convert.1
  38.5 16.4 %all-to-all-done = bf16[16,128,2,128]{3,0,2,1:T(8,128)(2,1)} async-done(((bf16[16,128,2,128]{3,0,2,1:T(8,128)(2,1)}), bf16[16,128,2,128]{3,0,2,1:T(8,128)(2,1)}, u32[]{:S(2)}, u32[]{:S(2)}) %all-to-all-start) | async-done | bytes 1048608 | tf_op jit(solution)/shard_map/all_to_all | solution.py:43
  54.9 1.6 %copy.32 = bf16[32,16,4,2,128]{4,1,0,3,2:T(8,128)(2,1)S(1)} copy(bf16[32,16,4,2,128]{4,1,3,2,0:T(8,128)(2,1)} %bitcast.7) | data formatting | bytes 2097152 | tf_op jit(solution)/shard_map/all_to_all | solution.py:43
  56.5 0.3 copy-done.2
  56.8 2.6 %fusion.31 = f32[4,1024,128]{1,2,0:T(8,128)} fusion(bf16[512,4,2,128]{3,0,2,1:T(8,128)(2,1)S(1)} %bitcast.86, bf16[1,1024,512]{2,1,0:T(8,128)(2,1)S(1)} %copy-done.1, bf16[1,1024,512]{2,1,0:T(8,128)(2,1)S(1)} %copy-done.2), kind=kOutput, calls=%fused_computation.39 | convolution fusion | flops 1074790400 | bytes 5242880 | tf_op jit(solution)/shard_map/qtk,ksqc->stc/dot_general | solution.py:40
  59.4 2.9 %copy.34 = f32[4,1024,128]{2,1,0:T(8,128)} copy(f32[4,1024,128]{1,2,0:T(8,128)} %fusion.31) | data formatting | bytes 4194304 | tf_op jit(solution)/shard_map/qtk,ksqc->stc/transpose | solution.py:40
  62.3 2.9 %copy.35 = f32[4096,128]{0,1:T(8,128)} copy(f32[4096,128]{1,0:T(8,128)} %bitcast.85) | data formatting | bytes 4194304 | tf_op jit(solution)/shard_map/reshape | solution.py:46
  65.3 51.2 %all-reduce.3.cloned.1.call-done = (bf16[128,128]{1,0:T(8,128)(2,1)}, bf16[128,128]{1,0:T(8,128)(2,1)}, bf16[128,128]{1,0:T(8,128)(2,1)}) async-done(((bf16[128,128]{1,0:T(8,128)(2,1)}, bf16[128,128]{1,0:T(8,128)(2,1)}, bf16[128,128]{1,0:T(8,128)(2,1)}), (bf16[128,128]{1,0:T(8,128)(2,1)}, bf16[128,128]{1,0:T(8,128)(2,1)}, bf16[128,128]{1,0:T(8,128)(2,1)})) %all-reduce.3.cloned.1.call-update) | async-done | bytes 98320 | tf_op jit(solution)/shard_map/psum | solution.py:16
  116.5 4.0 %convolution_convert_fusion = bf16[4096,128]{1,0:T(8,128)(2,1)} fusion(bf16[128,128]{1,0:T(8,128)(2,1)S(1)} %copy-done.4, f32[4096,128]{0,1:T(8,128)} %copy.35, bf16[4096,384]{1,0:T(8,128)(2,1)S(1)} %copy-done, bf16[128,128]{1,0:T(8,128)(2,1)} %get-tuple-element.5, bf16[128,128]{1,0:T(8,128)(2,1)} %get-tuple-element.6, bf16[128,128]{1,0:T(8,128)(2,1)} %get-tuple-element.7), kind=kOutput, calls=%fused_computation.3 | convolution fusion | flops 538738688 | bytes 6422528 | tf_op jit(solution)/shard_map/dot_general | solution.py:56
  (11 shorter events, 0.0 us)
Async XLA Ops:
  6.5 109.9 %copy-start = (bf16[4096,384]{1,0:T(8,128)(2,1)S(1)}, bf16[4096,384]{1,0:T(8,128)(2,1)}, u32[]{:S(2)}) copy-start(bf16[4096,384]{1,0:T(8,128)(2,1)} %param.8) | copy-start | bytes 9437188
  6.5 3.6 %copy-start.6 = (bf16[16,2,512,128]{3,2,1,0:T(8,128)(2,1)S(1)}, bf16[16,2,512,128]{3,2,1,0:T(8,128)(2,1)}, u32[]{:S(2)}) copy-start(bf16[16,2,512,128]{3,2,1,0:T(8,128)(2,1)} %param.7) | copy-start | bytes 12582916
  10.1 2.8 %copy-start.7 = (bf16[16,2,128,512]{3,2,1,0:T(8,128)(2,1)S(1)}, bf16[16,2,128,512]{3,2,1,0:T(8,128)(2,1)}, u32[]{:S(2)}) copy-start(bf16[16,2,128,512]{3,2,1,0:T(8,128)(2,1)} %param.6) | copy-start | bytes 12582916
  14.5 11.5 %copy-start.5 = (s32[3]{0:T(128)S(1)}, s32[3]{0:T(128)}, u32[]{:S(2)}) copy-start(s32[3]{0:T(128)} %param.10) | copy-start | bytes 40
  14.5 14.0 %copy-start.3 = (bf16[128,384]{1,0:T(8,128)(2,1)S(1)}, bf16[128,384]{1,0:T(8,128)(2,1)}, u32[]{:S(2)}) copy-start(bf16[128,384]{1,0:T(8,128)(2,1)} %param.9) | copy-start | bytes 294916
  16.1 38.8 %all-to-all-start = ((bf16[16,128,2,128]{3,0,2,1:T(8,128)(2,1)}), bf16[16,128,2,128]{3,0,2,1:T(8,128)(2,1)}, u32[]{:S(2)}, u32[]{:S(2)}) async-start(bf16[16,128,2,128]{3,0,2,1:T(8,128)(2,1)} %copy.31), calls=%async_computation | async-start | bytes 2097152 | tf_op jit(solution)/shard_map/all_to_all | solution.py:43
  25.9 90.6 %all-reduce.3.cloned.1.call-start = ((), (), s32[]{:S(2)}) async-start(), calls=%async_computation.1 | async-start | bytes 196608 | tf_op jit(solution)/shard_map/psum | solution.py:16
  54.9 1.6 %copy-start.1 = (bf16[1,1024,512]{2,1,0:T(8,128)(2,1)S(1)}, bf16[1,1024,512]{2,1,0:T(8,128)(2,1)}, u32[]{:S(2)}) copy-start(bf16[1,1024,512]{2,1,0:T(8,128)(2,1)} %get-tuple-element.14) | copy-start | bytes 3145732
  54.9 1.9 %copy-start.2 = (bf16[1,1024,512]{2,1,0:T(8,128)(2,1)S(1)}, bf16[1,1024,512]{2,1,0:T(8,128)(2,1)}, u32[]{:S(2)}) copy-start(bf16[1,1024,512]{2,1,0:T(8,128)(2,1)} %get-tuple-element.15) | copy-start | bytes 3145732
  62.3 54.2 %copy-start.4 = (bf16[128,128]{1,0:T(8,128)(2,1)S(1)}, bf16[128,128]{1,0:T(8,128)(2,1)}, u32[]{:S(2)}) copy-start(bf16[128,128]{1,0:T(8,128)(2,1)} %param.11) | copy-start | bytes 98308
Sparse Core Ops, SparseCore 0:
  29.5 86.8 all-reduce.2
where the time goes:
time: 128 us; the launch traced here: 127 us
  waiting for transfers between devices  67.6 us (53%)
  between operations  15.4 us (12%)
  matrix products  13.6 us (11%)
  local copies, waits for them, and re-layouts  10.9 us (9%)
  other arithmetic  10.1 us (8%)
  starting transfers between devices  9.75 us (8%)
    psum x1, waiting for transfers between devices, broadcast(): return lax.psum(jnp.where(mine, value, jnp.zeros_like(value)), axis)  51.2 us
    all_to_all x1, waiting for transfers between devices, per_device(): lax.all_to_all(spectra, 'freq', split_axis=1, concat_axis=0, tiled=True)  16.4 us
    all_to_all x1, starting transfers between devices, per_device(): lax.all_to_all(spectra, 'freq', split_axis=1, concat_axis=0, tiled=True)  9.71 us
    another operation x1, other arithmetic  9.32 us
    dot_general x4, matrix products, product(): jnp.einsum('ksm,kmc->ksc', left, right, preferred_element_type=jnp.float32)  6.95 us
    dot_general x1, matrix products, per_device(): jnp.dot(reduced, inverse_factor, preferred_element_type=jnp.float32)  4.02 us
    reshape x1, local copies, waits for them, and re-layouts, per_device(): hessian = hessian.reshape(-1, hessian.shape[-1])  2.95 us
    transpose x1, local copies, waits for them, and re-layouts, per_device(): jnp.einsum('qtk,ksqc->stc', table, lax.all_to_all(spectra, 'freq', split_...  2.91 us
  transfers between devices with their start and end apart: 2, of which 2 were waited for; matrix products, arithmetic and copies ran while one was open for 16% of the time, Pallas kernels for 0%

commit v1 on v0

v1 whole, which is shorter than its diff:
```python
import math

import jax
import jax.numpy as jnp
import numpy as np
from jax import lax
from jax.experimental import pallas as pl
from jax.experimental.pallas import tpu as pltpu
from jax.sharding import PartitionSpec as P

C = 128
M = 512
NF = 512
PANELS = 3
NT = 1024
NS = 1024
N_GRP = 8
N_FREQ = 32
KL = NF // N_FREQ
SL = NS // N_GRP
SD = SL // N_FREQ
K_STEP = 4
T_STEP = 256


def table_columns():
    phases = np.arange(NT)[:, None] * np.arange(NF)[None, :] % NT * (2.0 * math.pi / NT)
    table = np.stack([np.cos(phases), -np.sin(phases)], axis=1) / math.sqrt(NF)
    table = table.reshape(NT, 2, N_FREQ, KL).transpose(0, 2, 1, 3).reshape(NT, 2 * NF)
    return table.astype(jnp.bfloat16)


def spectra_kernel(transfer_ref, adjoint_ref, out_ref, rows_ref):
    step = pl.program_id(0)
    for j in range(K_STEP):
        left = transfer_ref[j].reshape(2 * SL, M)
        right = jnp.concatenate([adjoint_ref[j, 0], adjoint_ref[j, 1]], axis=1)
        full = jnp.dot(left, right, preferred_element_type=jnp.float32)
        k = step * K_STEP + j
        rows_ref[pl.ds(k, SL, stride=2 * KL), :] = full[:SL, :C] - full[SL:, C:]
        rows_ref[pl.ds(KL + k, SL, stride=2 * KL), :] = full[:SL, C:] + full[SL:, :C]

    @pl.when(step == KL // K_STEP - 1)
    def _():
        out_ref[...] = rows_ref[...].astype(jnp.bfloat16)


def spectra_rows(transfer, adjoint):
    return pl.pallas_call(
        spectra_kernel,
        grid=(KL // K_STEP,),
        in_specs=[
            pl.BlockSpec((K_STEP, 2, SL, M), lambda i: (i, 0, 0, 0)),
            pl.BlockSpec((K_STEP, 2, M, C), lambda i: (i, 0, 0, 0)),
        ],
        out_specs=pl.BlockSpec((SL * 2 * KL, C), lambda i: (0, 0)),
        out_shape=jax.ShapeDtypeStruct((SL * 2 * KL, C), jnp.bfloat16),
        scratch_shapes=[pltpu.VMEM((SL * 2 * KL, C), jnp.float32)],
        compiler_params=pltpu.CompilerParams(vmem_limit_bytes=32 * 2**20),
        name="spectra",
    )(transfer, adjoint)


def panel_kernel(table_ref, recv_ref, lower_ref, pivots_ref, inverse_ref, out_ref):
    table = table_ref[...]
    pivots = pivots_ref[...]
    inverse = inverse_ref[...]
    for pair in range(SD // 2):
        cols = [recv_ref[:, 2 * pair + i].reshape(2 * NF, C) for i in range(2)]
        both = jnp.dot(table, jnp.concatenate(cols, axis=1), preferred_element_type=jnp.float32)
        for i in range(2):
            s = 2 * pair + i
            update = lax.dot_general(
                lower_ref[s], pivots, (((1,), (1,)), ((), ())), preferred_element_type=jnp.float32
            )
            reduced = (both[:, i * C : (i + 1) * C] - update).astype(jnp.bfloat16)
            out_ref[s] = jnp.dot(reduced, inverse, preferred_element_type=jnp.float32).astype(jnp.bfloat16)


def panel_rows(table, recv, lower, pivots, inverse):
    return pl.pallas_call(
        panel_kernel,
        grid=(NT // T_STEP,),
        in_specs=[
            pl.BlockSpec((T_STEP, 2 * NF), lambda i: (i, 0)),
            pl.BlockSpec((N_FREQ, SD, 2 * KL, C), lambda i: (0, 0, 0, 0)),
            pl.BlockSpec((SD, T_STEP, PANELS * C), lambda i: (0, i, 0)),
            pl.BlockSpec((C, PANELS * C), lambda i: (0, 0)),
            pl.BlockSpec((C, C), lambda i: (0, 0)),
        ],
        out_specs=pl.BlockSpec((SD, T_STEP, C), lambda i: (0, i, 0)),
        out_shape=jax.ShapeDtypeStruct((SD, NT, C), jnp.bfloat16),
        compiler_params=pltpu.CompilerParams(vmem_limit_bytes=32 * 2**20),
        name="panel",
    )(table, recv, lower, pivots, inverse)


def gather_pivots(pivot_store, owners):
    mine = jnp.repeat(owners == lax.axis_index("grp"), C)[None, :]
    value = jnp.where(mine, pivot_store, jnp.zeros_like(pivot_store))
    for bit in (1, 2, 4):
        value = value + lax.ppermute(value, "grp", [(g, g ^ bit) for g in range(N_GRP)])
    return value


def per_device(transfer, adjoint, lower_rows, pivot_store, owners, inverse_factor):
    rows = spectra_rows(transfer, adjoint)
    recv = lax.all_to_all(rows.reshape(N_FREQ, SD, 2 * KL, C), "freq", split_axis=0, concat_axis=0, tiled=True)
    pivots = gather_pivots(pivot_store, owners)
    table = jnp.asarray(table_columns())
    out = panel_rows(table, recv, lower_rows.reshape(SD, NT, PANELS * C), pivots, inverse_factor)
    return out.reshape(SD * NT, C)


def solution(mesh):
    in_specs = (
        P("freq", None, "grp", None),
        P("freq", None, None, None),
        P(("grp", "freq"), None),
        P("grp", None),
        P(),
        P(),
    )
    out_specs = P(("grp", "freq"), None)
    return jax.shard_map(
        per_device, mesh=mesh, in_specs=in_specs, out_specs=out_specs, check_vma=False
    )
```

time: 128 us -> 55 us (0.43)
  the two profiles are of different devices: /device:TPU:32 before, /device:TPU:8 now
where the time goes in v1:
time: 55 us; the launch traced here: 54.2 us
  waiting for transfers between devices  22.4 us (41%)
  starting transfers between devices  15.5 us (28%)
  Pallas kernels  9.72 us (18%)
  local copies, waits for them, and re-layouts  6.35 us (12%)
    ppermute x3, waiting for transfers between devices, gather_pivots(): lax.ppermute(value, 'grp', [(g, g ^ bit) for g in range(N_GRP)])  12.5 us
    all_to_all x1, waiting for transfers between devices, per_device(): lax.all_to_all(rows.reshape(N_FREQ, SD, 2 * KL, C), 'freq', split_axis=0,...  9.88 us
    all_to_all x1, starting transfers between devices, per_device(): lax.all_to_all(rows.reshape(N_FREQ, SD, 2 * KL, C), 'freq', split_axis=0,...  9.78 us
    unnamed x14, local copies, waits for them, and re-layouts  6.28 us
    pallas_call x1, Pallas kernels, panel_rows(): pl.pallas_call(panel_kernel, grid=(NT // T_STEP,), in_specs=[pl.BlockSpec...  5.95 us
    ppermute x3, starting transfers between devices, gather_pivots(): lax.ppermute(value, 'grp', [(g, g ^ bit) for g in range(N_GRP)])  5.74 us
    pallas_call x1, Pallas kernels, spectra_rows(): pl.pallas_call(spectra_kernel, grid=(KL // K_STEP,), in_specs=[pl.BlockSp...  3.77 us
  transfers between devices with their start and end apart: 4, of which 4 were waited for; matrix products, arithmetic and copies ran while one was open for 0% of the time, Pallas kernels for 0%

profile of v1, /device:TPU:8, one launch (start us, length us, event | category | flops | bytes accessed | tf_op | source)
XLA Modules:
  0.0 54.2 jit_solution(7568135539028761185)
XLA Ops:
  0.0 0.0 copy-start
  0.0 2.2 %copy-done = bf16[16,2,128,512]{3,2,1,0:T(8,128)(2,1)S(1)} copy-done((bf16[16,2,128,512]{3,2,1,0:T(8,128)(2,1)S(1)}, bf16[16,2,128,512]{3,2,1,0:T(8,128)(2,1)}, u32[]{:S(2)}) %copy-start) | copy-done | bytes 4194328
  2.2 0.0 copy-start.1
  2.2 2.2 %copy-done.1 = bf16[16,2,512,128]{3,2,1,0:T(8,128)(2,1)S(1)} copy-done((bf16[16,2,512,128]{3,2,1,0:T(8,128)(2,1)S(1)}, bf16[16,2,512,128]{3,2,1,0:T(8,128)(2,1)}, u32[]{:S(2)}) %copy-start.1) | copy-done | bytes 4194328
  4.4 0.0 copy-start.6
  4.4 0.0 copy-start.5
  4.4 0.0 copy-start.3
  4.4 0.0 copy-start.4
  4.4 3.8 %spectra.1 = bf16[4096,128]{1,0:T(8,128)(2,1)} custom-call(bf16[16,2,128,512]{3,2,1,0:T(8,128)(2,1)S(1)} %copy-done, bf16[16,2,512,128]{3,2,1,0:T(8,128)(2,1)S(1)} %copy-done.1), custom_call_target="tpu_custom_call" | custom-call | tf_op jit(solution)/shard_map/spectra/pallas_call | solution.py:49
  8.2 9.8 %all-to-all-start = ((bf16[32,4,32,128]{3,2,1,0:T(8,128)(2,1)}), bf16[32,4,32,128]{3,2,1,0:T(8,128)(2,1)S(1)}, u32[]{:S(2)}, u32[]{:S(2)}) async-start(bf16[32,4,32,128]{3,2,1,0:T(8,128)(2,1)} %bitcast), calls=%async_computation | async-start | bytes 2097152 | tf_op jit(solution)/shard_map/all_to_all | solution.py:108
  18.0 0.0 copy-done.6
  18.0 0.1 broadcast_bitcast_fusion
  18.0 0.0 copy-done.5
  18.1 0.5 collective-permute-start
  18.6 4.5 %collective-permute-done = bf16[128,384]{1,0:T(8,128)(2,1)S(1)} collective-permute-done((bf16[128,384]{1,0:T(8,128)(2,1)S(1)}, bf16[128,384]{1,0:T(8,128)(2,1)S(1)}, u32[]{:S(2)}, u32[]{:S(2)}) %collective-permute-start) | collective-permute-done | bytes 98336 | tf_op jit(solution)/shard_map/ppermute | solution.py:102
  23.2 2.4 %collective-permute-start.1 = (bf16[128,384]{1,0:T(8,128)(2,1)S(1)}, bf16[128,384]{1,0:T(8,128)(2,1)S(1)}, u32[]{:S(2)}, u32[]{:S(2)}) collective-permute-start(bf16[128,384]{1,0:T(8,128)(2,1)S(1)} %fusion), channel_id=1, source_target_pairs={{0,64},{32,96},{64,0},{96,32},{128,192},{160,224},{192,128},{224,1... | collective-permute-start | bytes 294920 | tf_op jit(solution)/shard_map/ppermute | solution.py:102
  25.5 3.8 %collective-permute-done.1 = bf16[128,384]{1,0:T(8,128)(2,1)S(1)} collective-permute-done((bf16[128,384]{1,0:T(8,128)(2,1)S(1)}, bf16[128,384]{1,0:T(8,128)(2,1)S(1)}, u32[]{:S(2)}, u32[]{:S(2)}) %collective-permute-start.1) | collective-permute-done | bytes 98336 | tf_op jit(solution)/shard_map/ppermute | solution.py:102
  29.4 2.8 %collective-permute-start.2 = (bf16[128,384]{1,0:T(8,128)(2,1)S(1)}, bf16[128,384]{1,0:T(8,128)(2,1)S(1)}, u32[]{:S(2)}, u32[]{:S(2)}) collective-permute-start(bf16[128,384]{1,0:T(8,128)(2,1)S(1)} %add.10), channel_id=1, source_target_pairs={{0,128},{32,160},{64,192},{96,224},{128,0},{160,32},{192,64},{224,... | collective-permute-start | bytes 294920 | tf_op jit(solution)/shard_map/ppermute | solution.py:102
  32.2 4.2 %collective-permute-done.2 = bf16[128,384]{1,0:T(8,128)(2,1)S(1)} collective-permute-done((bf16[128,384]{1,0:T(8,128)(2,1)S(1)}, bf16[128,384]{1,0:T(8,128)(2,1)S(1)}, u32[]{:S(2)}, u32[]{:S(2)}) %collective-permute-start.2) | collective-permute-done | bytes 98336 | tf_op jit(solution)/shard_map/ppermute | solution.py:102
  36.4 9.9 %all-to-all-done.recv_ref = bf16[32,4,32,128]{3,2,1,0:T(8,128)(2,1)S(1)} async-done(((bf16[32,4,32,128]{3,2,1,0:T(8,128)(2,1)}), bf16[32,4,32,128]{3,2,1,0:T(8,128)(2,1)S(1)}, u32[]{:S(2)}, u32[]{:S(2)}) %all-to-all-start) | async-done | bytes 1048608 | tf_op jit(solution)/shard_map/all_to_all | solution.py:108
  46.3 0.0 copy-done.3
  46.3 0.0 copy-done.4
  46.3 1.9 %copy-done.2 = bf16[4096,384]{1,0:T(8,128)(2,1)S(1)} copy-done((bf16[4096,384]{1,0:T(8,128)(2,1)S(1)}, bf16[4096,384]{1,0:T(8,128)(2,1)}, u32[]{:S(2)}) %copy-start.2) | copy-done | bytes 3145752
  48.2 6.0 %panel.1 = bf16[4,1024,128]{2,1,0:T(8,128)(2,1)} custom-call(bf16[1024,1024]{1,0:T(8,128)(2,1)S(1)} %copy-done.3, bf16[32,4,32,128]{3,2,1,0:T(8,128)(2,1)S(1)} %all-to-all-done.recv_ref, bf16[4,1024,384]{2,1,0:T(8,128)(2,1)S(1)} %bitcast.5, bf16[128,384]{1,0:T(8,128)(2,1)S(1)} %add.11.pivots_ref, bf16[128,128]{1,0:T(8,128)(2,1)S(1)} %copy-done.4), custom_call_target="tpu_custom_call" | custom-call | tf_op jit(solution)/shard_map/panel/pallas_call | solution.py:81
  (6 shorter events, 0.1 us)
Async XLA Ops:
  0.0 2.2 %copy-start = (bf16[16,2,128,512]{3,2,1,0:T(8,128)(2,1)S(1)}, bf16[16,2,128,512]{3,2,1,0:T(8,128)(2,1)}, u32[]{:S(2)}) copy-start(bf16[16,2,128,512]{3,2,1,0:T(8,128)(2,1)} %transfer_ref.1) | copy-start | bytes 12582916
  2.2 2.2 %copy-start.1 = (bf16[16,2,512,128]{3,2,1,0:T(8,128)(2,1)S(1)}, bf16[16,2,512,128]{3,2,1,0:T(8,128)(2,1)}, u32[]{:S(2)}) copy-start(bf16[16,2,512,128]{3,2,1,0:T(8,128)(2,1)} %adjoint_ref.1) | copy-start | bytes 12582916
  4.4 13.6 %copy-start.6 = (s32[3]{0:T(128)S(1)}, s32[3]{0:T(128)}, u32[]{:S(2)}) copy-start(s32[3]{0:T(128)} %param.11) | copy-start | bytes 40
  4.4 13.7 %copy-start.5 = (bf16[128,384]{1,0:T(8,128)(2,1)S(1)}, bf16[128,384]{1,0:T(8,128)(2,1)}, u32[]{:S(2)}) copy-start(bf16[128,384]{1,0:T(8,128)(2,1)} %param.10) | copy-start | bytes 294916
  4.4 41.9 %copy-start.3 = (bf16[1024,1024]{1,0:T(8,128)(2,1)S(1)}, bf16[1024,1024]{1,0:T(8,128)(2,1)}, u32[]{:S(2)}) copy-start(bf16[1024,1024]{1,0:T(8,128)(2,1)} %constant.10.clone.table_ref) | copy-start | bytes 6291460
  4.4 41.9 %copy-start.4 = (bf16[128,128]{1,0:T(8,128)(2,1)S(1)}, bf16[128,128]{1,0:T(8,128)(2,1)}, u32[]{:S(2)}) copy-start(bf16[128,128]{1,0:T(8,128)(2,1)} %inverse_ref.1) | copy-start | bytes 98308
  8.2 38.2 %all-to-all-start = ((bf16[32,4,32,128]{3,2,1,0:T(8,128)(2,1)}), bf16[32,4,32,128]{3,2,1,0:T(8,128)(2,1)S(1)}, u32[]{:S(2)}, u32[]{:S(2)}) async-start(bf16[32,4,32,128]{3,2,1,0:T(8,128)(2,1)} %bitcast), calls=%async_computation | async-start | bytes 2097152 | tf_op jit(solution)/shard_map/all_to_all | solution.py:108
  18.1 5.1 %collective-permute-start = (bf16[128,384]{1,0:T(8,128)(2,1)S(1)}, bf16[128,384]{1,0:T(8,128)(2,1)S(1)}, u32[]{:S(2)}, u32[]{:S(2)}) collective-permute-start(bf16[128,384]{1,0:T(8,128)(2,1)S(1)} %broadcast_select_fusion), channel_id=1, source_target_pairs={{0,32},{32,0},{64,96},{96,64},{128,160},{160,128},{192,224},{224,1... | collective-permute-start | bytes 294920 | tf_op jit(solution)/shard_map/ppermute | solution.py:102
  23.2 6.2 %collective-permute-start.1 = (bf16[128,384]{1,0:T(8,128)(2,1)S(1)}, bf16[128,384]{1,0:T(8,128)(2,1)S(1)}, u32[]{:S(2)}, u32[]{:S(2)}) collective-permute-start(bf16[128,384]{1,0:T(8,128)(2,1)S(1)} %fusion), channel_id=1, source_target_pairs={{0,64},{32,96},{64,0},{96,32},{128,192},{160,224},{192,128},{224,1... | collective-permute-start | bytes 294920 | tf_op jit(solution)/shard_map/ppermute | solution.py:102
  29.4 7.0 %collective-permute-start.2 = (bf16[128,384]{1,0:T(8,128)(2,1)S(1)}, bf16[128,384]{1,0:T(8,128)(2,1)S(1)}, u32[]{:S(2)}, u32[]{:S(2)}) collective-permute-start(bf16[128,384]{1,0:T(8,128)(2,1)S(1)} %add.10), channel_id=1, source_target_pairs={{0,128},{32,160},{64,192},{96,224},{128,0},{160,32},{192,64},{224,... | collective-permute-start | bytes 294920 | tf_op jit(solution)/shard_map/ppermute | solution.py:102
  46.3 1.9 %copy-start.2 = (bf16[4096,384]{1,0:T(8,128)(2,1)S(1)}, bf16[4096,384]{1,0:T(8,128)(2,1)}, u32[]{:S(2)}) copy-start(bf16[4096,384]{1,0:T(8,128)(2,1)} %param.9) | copy-start | bytes 9437188

commit v2 on v1

v2 whole, which is shorter than its diff:
```python
import math

import jax
import jax.numpy as jnp
import numpy as np
from jax import lax
from jax.experimental import pallas as pl
from jax.experimental.pallas import tpu as pltpu
from jax.sharding import PartitionSpec as P

C = 128
M = 512
NF = 512
PANELS = 3
NT = 1024
NS = 1024
N_GRP = 8
N_FREQ = 32
KL = NF // N_FREQ
SL = NS // N_GRP
SD = SL // N_FREQ
ROWS = 2 * KL
PITCH = ROWS + 1
CHUNKS = 8
HALF = NT // 2
T_CHUNK = 128


def table_halves():
    phases = np.arange(HALF)[:, None] * np.arange(NF)[None, :] % NT * (2.0 * math.pi / NT)
    table = np.stack([np.cos(phases), -np.sin(phases)], axis=1) / math.sqrt(NF)
    table = table.reshape(HALF, 2, N_FREQ, KL // 2, 2).transpose(4, 0, 2, 1, 3).reshape(2, HALF, NF)
    return table.astype(jnp.bfloat16)


def spectra_kernel(transfer_hbm, adjoint_hbm, out_ref, transfer_ref, adjoint_ref, rows_ref, sems):
    per = KL // CHUNKS
    copies = []
    for i in range(CHUNKS):
        part = pl.ds(i * per, per)
        for j, (src, dst) in enumerate(((transfer_hbm, transfer_ref), (adjoint_hbm, adjoint_ref))):
            copy = pltpu.make_async_copy(src.at[part], dst.at[part], sems.at[j, i])
            copy.start()
            copies.append(copy)
    for k in range(KL):
        if k % per == 0:
            copies[k // per * 2].wait()
            copies[k // per * 2 + 1].wait()
        left = transfer_ref[k].reshape(2 * SL, M)
        right = jnp.concatenate([adjoint_ref[k, 0], adjoint_ref[k, 1]], axis=1)
        full = jnp.dot(left, right, preferred_element_type=jnp.float32)
        row = k % 2 * KL + k // 2
        rows_ref[pl.ds(row, SL, stride=PITCH), :] = full[:SL, :C] - full[SL:, C:]
        rows_ref[pl.ds(row + KL // 2, SL, stride=PITCH), :] = full[:SL, C:] + full[SL:, :C]
    for s in range(SL):
        out_ref[pl.ds(s * ROWS, ROWS), :] = rows_ref[pl.ds(s * PITCH, ROWS), :].astype(jnp.bfloat16)


def spectra_rows(transfer, adjoint):
    return pl.pallas_call(
        spectra_kernel,
        in_specs=[pl.BlockSpec(memory_space=pl.ANY)] * 2,
        out_specs=pl.BlockSpec(memory_space=pltpu.VMEM),
        out_shape=jax.ShapeDtypeStruct((SL * ROWS, C), jnp.bfloat16),
        scratch_shapes=[
            pltpu.VMEM((KL, 2, SL, M), jnp.bfloat16),
            pltpu.VMEM((KL, 2, M, C), jnp.bfloat16),
            pltpu.VMEM((SL * PITCH + PITCH + 7, C), jnp.float32),
            pltpu.SemaphoreType.DMA((2, CHUNKS)),
        ],
        compiler_params=pltpu.CompilerParams(vmem_limit_bytes=60 * 2**20),
        name="spectra",
    )(transfer, adjoint)


def update_kernel(lower_ref, pivots_ref, out_ref):
    out_ref[...] = lax.dot_general(
        lower_ref[...], pivots_ref[...], (((1,), (1,)), ((), ())), preferred_element_type=jnp.float32
    )


def update_rows(lower, pivots):
    rows = lower.shape[0]
    step = rows // 4
    return pl.pallas_call(
        update_kernel,
        grid=(rows // step,),
        in_specs=[
            pl.BlockSpec((step, PANELS * C), lambda i: (i, 0)),
            pl.BlockSpec((C, PANELS * C), lambda i: (0, 0)),
        ],
        out_specs=pl.BlockSpec((step, C), lambda i: (i, 0)),
        out_shape=jax.ShapeDtypeStruct((rows, C), jnp.float32),
        compiler_params=pltpu.CompilerParams(vmem_limit_bytes=16 * 2**20),
        cost_estimate=pl.CostEstimate(
            flops=2 * rows * PANELS * C * C, bytes_accessed=rows * (PANELS * C * 2 + C * 4), transcendentals=0
        ),
        name="update",
    )(lower, pivots)


def panel_kernel(table_ref, recv_ref, update_ref, inverse_ref, out_hbm, out_ref, sems):
    inverse = inverse_ref[...]
    sides = []
    for parity in range(2):
        cols = [recv_ref[:, s, parity].reshape(NF, C) for s in range(SD)]
        sides.append(jnp.concatenate(cols, axis=1))
    copies = []
    for i in range(HALF // T_CHUNK):
        part = pl.ds(i * T_CHUNK, T_CHUNK)
        even = jnp.dot(table_ref[0, part], sides[0], preferred_element_type=jnp.float32)
        odd = jnp.dot(table_ref[1, part], sides[1], preferred_element_type=jnp.float32)
        for half, sums in enumerate((even + odd, even - odd)):
            where = pl.ds(half * HALF + i * T_CHUNK, T_CHUNK)
            for s in range(SD):
                reduced = (sums[:, s * C : (s + 1) * C] - update_ref[s, where]).astype(jnp.bfloat16)
                out_ref[s, where] = jnp.dot(reduced, inverse, preferred_element_type=jnp.float32).astype(jnp.bfloat16)
            copy = pltpu.make_async_copy(out_ref.at[:, where], out_hbm.at[:, where], sems.at[2 * i + half])
            copy.start()
            copies.append(copy)
    for copy in copies:
        copy.wait()


def panel_rows(table, recv, update, inverse):
    return pl.pallas_call(
        panel_kernel,
        in_specs=[pl.BlockSpec(memory_space=pltpu.VMEM)] * 4,
        out_specs=pl.BlockSpec(memory_space=pl.ANY),
        out_shape=jax.ShapeDtypeStruct((SD, NT, C), jnp.bfloat16),
        scratch_shapes=[
            pltpu.VMEM((SD, NT, C), jnp.bfloat16),
            pltpu.SemaphoreType.DMA((2 * HALF // T_CHUNK,)),
        ],
        compiler_params=pltpu.CompilerParams(vmem_limit_bytes=24 * 2**20),
        name="panel",
    )(table, recv, update, inverse)


def gather_pivots(pivot_store, owners):
    mine = jnp.repeat(owners == lax.axis_index("grp"), C)[None, :]
    value = jnp.where(mine, pivot_store, jnp.zeros_like(pivot_store))
    for bit in (1, 2, 4):
        value = value + lax.ppermute(value, "grp", [(g, g ^ bit) for g in range(N_GRP)])
    return value


def per_device(transfer, adjoint, lower_rows, pivot_store, owners, inverse_factor):
    rows = spectra_rows(transfer, adjoint)
    recv = lax.all_to_all(rows.reshape(N_FREQ, SD, 2, KL, C), "freq", split_axis=0, concat_axis=0, tiled=True)
    pivots = gather_pivots(pivot_store, owners)
    update = update_rows(lower_rows, pivots)
    table = jnp.asarray(table_halves())
    out = panel_rows(table, recv, update.reshape(SD, NT, C), inverse_factor)
    return out.reshape(SD * NT, C)


def solution(mesh):
    in_specs = (
        P("freq", None, "grp", None),
        P("freq", None, None, None),
        P(("grp", "freq"), None),
        P("grp", None),
        P(),
        P(),
    )
    out_specs = P(("grp", "freq"), None)
    return jax.shard_map(
        per_device, mesh=mesh, in_specs=in_specs, out_specs=out_specs, check_vma=False
    )
```

time: 55 us -> 47.5 us (0.86)
  waiting for transfers between devices: 22.4 us -> 19 us
  local copies, waits for them, and re-layouts: 6.35 us -> 3.2 us
  Pallas kernels: 9.72 us -> 8.76 us
    all_to_all x1, waiting for transfers between devices: 9.88 us -> 6.5 us  [per_device(): lax.all_to_all(rows.reshape(N_FREQ, SD, 2, KL, C), 'freq', split_axis=0,...]
    unnamed x14 -> x10, local copies, waits for them, and re-layouts: 6.28 us -> 3.12 us
    pallas_call x2 -> x3, Pallas kernels: 9.72 us -> 8.76 us  [the longest x1 4.93 us: spectra_rows(): pl.pallas_call(spectra_kernel, in_specs=[pl.BlockSpec(memory_space=pl.ANY...]
  transfers between devices with their start and end apart: 4 -> 4, of which waited for: 4 -> 4; matrix products, arithmetic and copies ran while one was open for 0% -> 0% of each run, Pallas kernels for 0% -> 3%
where the time goes in v2:
time: 47.5 us; the launch traced here: 46.7 us
  waiting for transfers between devices  19 us (40%)
  starting transfers between devices  15.5 us (33%)
  Pallas kernels  8.76 us (18%)
  local copies, waits for them, and re-layouts  3.2 us (7%)
    ppermute x3, waiting for transfers between devices, gather_pivots(): lax.ppermute(value, 'grp', [(g, g ^ bit) for g in range(N_GRP)])  12.5 us
    all_to_all x1, starting transfers between devices, per_device(): lax.all_to_all(rows.reshape(N_FREQ, SD, 2, KL, C), 'freq', split_axis=0,...  9.79 us
    all_to_all x1, waiting for transfers between devices, per_device(): lax.all_to_all(rows.reshape(N_FREQ, SD, 2, KL, C), 'freq', split_axis=0,...  6.5 us
    ppermute x3, starting transfers between devices, gather_pivots(): lax.ppermute(value, 'grp', [(g, g ^ bit) for g in range(N_GRP)])  5.74 us
    pallas_call x1, Pallas kernels, spectra_rows(): pl.pallas_call(spectra_kernel, in_specs=[pl.BlockSpec(memory_space=pl.ANY...  4.93 us
    unnamed x10, local copies, waits for them, and re-layouts  3.12 us
    pallas_call x1, Pallas kernels, panel_rows(): pl.pallas_call(panel_kernel, in_specs=[pl.BlockSpec(memory_space=pltpu.VM...  2.35 us
    pallas_call x1, Pallas kernels, update_rows(): pl.pallas_call(update_kernel, grid=(rows // step,), in_specs=[pl.BlockSpe...  1.48 us
  transfers between devices with their start and end apart: 4, of which 4 were waited for; matrix products, arithmetic and copies ran while one was open for 0% of the time, Pallas kernels for 3%

profile of v2, /device:TPU:8, one launch (start us, length us, event | category | flops | bytes accessed | tf_op | source)
XLA Modules:
  0.0 46.7 jit_solution(16729881194288319528)
XLA Ops:
  0.0 0.0 copy-start.4
  0.0 0.0 copy-start.3
  0.0 4.9 %spectra.1 = bf16[4096,128]{1,0:T(8,128)(2,1)} custom-call(bf16[16,2,128,512]{3,2,1,0:T(8,128)(2,1)} %transfer_hbm.1, bf16[16,2,512,128]{3,2,1,0:T(8,128)(2,1)} %adjoint_hbm.1), custom_call_target="tpu_custom_call" | custom-call | tf_op jit(solution)/shard_map/spectra/pallas_call | solution.py:60
  4.9 0.0 copy-start.2
  5.0 9.8 %all-to-all-start = ((bf16[32,4,2,16,128]{4,3,2,1,0:T(8,128)(2,1)}), bf16[32,4,2,16,128]{4,3,2,1,0:T(8,128)(2,1)S(1)}, u32[]{:S(2)}, u32[]{:S(2)}) async-start(bf16[32,4,2,16,128]{4,3,2,1,0:T(8,128)(2,1)} %bitcast.6), calls=%async_computation | async-start | bytes 2097152 | tf_op jit(solution)/shard_map/all_to_all | solution.py:150
  14.8 0.0 copy-done.4
  14.8 0.1 broadcast_bitcast_fusion
  14.9 0.0 copy-done.3
  14.9 0.5 %collective-permute-start = (bf16[128,384]{1,0:T(8,128)(2,1)S(1)}, bf16[128,384]{1,0:T(8,128)(2,1)S(1)}, u32[]{:S(2)}, u32[]{:S(2)}) collective-permute-start(bf16[128,384]{1,0:T(8,128)(2,1)S(1)} %broadcast_select_fusion), channel_id=1, source_target_pairs={{0,32},{32,0},{64,96},{96,64},{128,160},{160,128},{192,224},{224,1... | collective-permute-start | bytes 294920 | tf_op jit(solution)/shard_map/ppermute | solution.py:144
  15.4 4.5 %collective-permute-done = bf16[128,384]{1,0:T(8,128)(2,1)S(1)} collective-permute-done((bf16[128,384]{1,0:T(8,128)(2,1)S(1)}, bf16[128,384]{1,0:T(8,128)(2,1)S(1)}, u32[]{:S(2)}, u32[]{:S(2)}) %collective-permute-start) | collective-permute-done | bytes 98336 | tf_op jit(solution)/shard_map/ppermute | solution.py:144
  20.0 2.4 %collective-permute-start.1 = (bf16[128,384]{1,0:T(8,128)(2,1)S(1)}, bf16[128,384]{1,0:T(8,128)(2,1)S(1)}, u32[]{:S(2)}, u32[]{:S(2)}) collective-permute-start(bf16[128,384]{1,0:T(8,128)(2,1)S(1)} %fusion), channel_id=1, source_target_pairs={{0,64},{32,96},{64,0},{96,32},{128,192},{160,224},{192,128},{224,1... | collective-permute-start | bytes 294920 | tf_op jit(solution)/shard_map/ppermute | solution.py:144
  22.4 3.8 %collective-permute-done.1 = bf16[128,384]{1,0:T(8,128)(2,1)S(1)} collective-permute-done((bf16[128,384]{1,0:T(8,128)(2,1)S(1)}, bf16[128,384]{1,0:T(8,128)(2,1)S(1)}, u32[]{:S(2)}, u32[]{:S(2)}) %collective-permute-start.1) | collective-permute-done | bytes 98336 | tf_op jit(solution)/shard_map/ppermute | solution.py:144
  26.2 2.8 %collective-permute-start.2 = (bf16[128,384]{1,0:T(8,128)(2,1)S(1)}, bf16[128,384]{1,0:T(8,128)(2,1)S(1)}, u32[]{:S(2)}, u32[]{:S(2)}) collective-permute-start(bf16[128,384]{1,0:T(8,128)(2,1)S(1)} %add.10), channel_id=1, source_target_pairs={{0,128},{32,160},{64,192},{96,224},{128,0},{160,32},{192,64},{224,... | collective-permute-start | bytes 294920 | tf_op jit(solution)/shard_map/ppermute | solution.py:144
  29.0 4.2 %collective-permute-done.2 = bf16[128,384]{1,0:T(8,128)(2,1)S(1)} collective-permute-done((bf16[128,384]{1,0:T(8,128)(2,1)S(1)}, bf16[128,384]{1,0:T(8,128)(2,1)S(1)}, u32[]{:S(2)}, u32[]{:S(2)}) %collective-permute-start.2) | collective-permute-done | bytes 98336 | tf_op jit(solution)/shard_map/ppermute | solution.py:144
  33.2 0.0 copy-start
  33.3 1.9 %copy-done = bf16[4096,384]{1,0:T(8,128)(2,1)S(1)} copy-done((bf16[4096,384]{1,0:T(8,128)(2,1)S(1)}, bf16[4096,384]{1,0:T(8,128)(2,1)}, u32[]{:S(2)}) %copy-start) | copy-done | bytes 3145752
  35.1 1.5 %update.1 = f32[4096,128]{1,0:T(8,128)S(1)} custom-call(bf16[4096,384]{1,0:T(8,128)(2,1)S(1)} %copy-done, bf16[128,384]{1,0:T(8,128)(2,1)S(1)} %add.11.pivots_ref), custom_call_target="tpu_custom_call" | custom-call | flops 402653184 | bytes 5242880 | tf_op jit(solution)/shard_map/update/pallas_call | solution.py:85
  36.6 6.5 %all-to-all-done.recv_ref = bf16[32,4,2,16,128]{4,3,2,1,0:T(8,128)(2,1)S(1)} async-done(((bf16[32,4,2,16,128]{4,3,2,1,0:T(8,128)(2,1)}), bf16[32,4,2,16,128]{4,3,2,1,0:T(8,128)(2,1)S(1)}, u32[]{:S(2)}, u32[]{:S(2)}) %all-to-all-start) | async-done | bytes 1048608 | tf_op jit(solution)/shard_map/all_to_all | solution.py:150
  43.1 0.0 copy-done.2
  43.1 0.0 copy-start.1
  43.1 1.2 %copy-done.1 = bf16[2,512,512]{2,1,0:T(8,128)(2,1)S(1)} copy-done((bf16[2,512,512]{2,1,0:T(8,128)(2,1)S(1)}, bf16[2,512,512]{2,1,0:T(8,128)(2,1)}, u32[]{:S(2)}) %copy-start.1) | copy-done | bytes 1048600
  44.4 2.4 %panel.1 = bf16[4,1024,128]{2,1,0:T(8,128)(2,1)} custom-call(bf16[2,512,512]{2,1,0:T(8,128)(2,1)S(1)} %copy-done.1, bf16[32,4,2,16,128]{4,3,2,1,0:T(8,128)(2,1)S(1)} %all-to-all-done.recv_ref, f32[4,1024,128]{2,1,0:T(8,128)S(1)} %bitcast.5, bf16[128,128]{1,0:T(8,128)(2,1)S(1)} %copy-done.2), custom_call_target="tpu_custom_call" | custom-call | tf_op jit(solution)/shard_map/panel/pallas_call | solution.py:126
  (5 shorter events, 0.1 us)
Async XLA Ops:
  0.0 14.8 %copy-start.4 = (s32[3]{0:T(128)S(1)}, s32[3]{0:T(128)}, u32[]{:S(2)}) copy-start(s32[3]{0:T(128)} %param.11) | copy-start | bytes 40
  0.0 14.9 %copy-start.3 = (bf16[128,384]{1,0:T(8,128)(2,1)S(1)}, bf16[128,384]{1,0:T(8,128)(2,1)}, u32[]{:S(2)}) copy-start(bf16[128,384]{1,0:T(8,128)(2,1)} %param.10) | copy-start | bytes 294916
  4.9 38.2 %copy-start.2 = (bf16[128,128]{1,0:T(8,128)(2,1)S(1)}, bf16[128,128]{1,0:T(8,128)(2,1)}, u32[]{:S(2)}) copy-start(bf16[128,128]{1,0:T(8,128)(2,1)} %inverse_ref.1) | copy-start | bytes 98308
  5.0 38.2 %all-to-all-start = ((bf16[32,4,2,16,128]{4,3,2,1,0:T(8,128)(2,1)}), bf16[32,4,2,16,128]{4,3,2,1,0:T(8,128)(2,1)S(1)}, u32[]{:S(2)}, u32[]{:S(2)}) async-start(bf16[32,4,2,16,128]{4,3,2,1,0:T(8,128)(2,1)} %bitcast.6), calls=%async_computation | async-start | bytes 2097152 | tf_op jit(solution)/shard_map/all_to_all | solution.py:150
  14.9 5.1 %collective-permute-start = (bf16[128,384]{1,0:T(8,128)(2,1)S(1)}, bf16[128,384]{1,0:T(8,128)(2,1)S(1)}, u32[]{:S(2)}, u32[]{:S(2)}) collective-permute-start(bf16[128,384]{1,0:T(8,128)(2,1)S(1)} %broadcast_select_fusion), channel_id=1, source_target_pairs={{0,32},{32,0},{64,96},{96,64},{128,160},{160,128},{192,224},{224,1... | collective-permute-start | bytes 294920 | tf_op jit(solution)/shard_map/ppermute | solution.py:144
  20.0 6.2 %collective-permute-start.1 = (bf16[128,384]{1,0:T(8,128)(2,1)S(1)}, bf16[128,384]{1,0:T(8,128)(2,1)S(1)}, u32[]{:S(2)}, u32[]{:S(2)}) collective-permute-start(bf16[128,384]{1,0:T(8,128)(2,1)S(1)} %fusion), channel_id=1, source_target_pairs={{0,64},{32,96},{64,0},{96,32},{128,192},{160,224},{192,128},{224,1... | collective-permute-start | bytes 294920 | tf_op jit(solution)/shard_map/ppermute | solution.py:144
  26.2 7.0 %collective-permute-start.2 = (bf16[128,384]{1,0:T(8,128)(2,1)S(1)}, bf16[128,384]{1,0:T(8,128)(2,1)S(1)}, u32[]{:S(2)}, u32[]{:S(2)}) collective-permute-start(bf16[128,384]{1,0:T(8,128)(2,1)S(1)} %add.10), channel_id=1, source_target_pairs={{0,128},{32,160},{64,192},{96,224},{128,0},{160,32},{192,64},{224,... | collective-permute-start | bytes 294920 | tf_op jit(solution)/shard_map/ppermute | solution.py:144
  33.2 1.9 %copy-start = (bf16[4096,384]{1,0:T(8,128)(2,1)S(1)}, bf16[4096,384]{1,0:T(8,128)(2,1)}, u32[]{:S(2)}) copy-start(bf16[4096,384]{1,0:T(8,128)(2,1)} %lower_ref.1) | copy-start | bytes 9437188
  43.1 1.2 %copy-start.1 = (bf16[2,512,512]{2,1,0:T(8,128)(2,1)S(1)}, bf16[2,512,512]{2,1,0:T(8,128)(2,1)}, u32[]{:S(2)}) copy-start(bf16[2,512,512]{2,1,0:T(8,128)(2,1)} %constant.10.clone.table_ref) | copy-start | bytes 3145732

commit v3 on v2

v3 whole, which is shorter than its diff:
```python
import math

import jax
import jax.numpy as jnp
import numpy as np
from jax import lax
from jax.experimental import pallas as pl
from jax.experimental.pallas import tpu as pltpu
from jax.sharding import PartitionSpec as P

C = 128
M = 512
NF = 512
PANELS = 3
NT = 1024
NS = 1024
N_GRP = 8
N_FREQ = 32
KL = NF // N_FREQ
SL = NS // N_GRP
SD = SL // N_FREQ
ROWS = 2 * KL
PITCH = ROWS + 1
LOADS = 4
HALF = NT // 2
T_STEP = HALF // 2
T_CHUNK = 128


def table_parts():
    phases = np.arange(HALF)[:, None] * np.arange(NF)[None, :] % NT * (2.0 * math.pi / NT)
    table = np.stack([np.cos(phases), -np.sin(phases)], axis=1) / math.sqrt(NF)
    table = table.reshape(HALF, 2, N_FREQ, KL // 2, 2).transpose(4, 0, 2, 1, 3).reshape(2, HALF, NF)
    return np.concatenate([table[0, : HALF // 2], table[1]]).astype(jnp.bfloat16)


def spectra_kernel(
    transfer_hbm, adjoint_hbm, out_hbm, transfer_ref, adjoint_ref, rows_ref, out_ref, load_sems, out_sems
):
    per = KL // 2 // LOADS
    loads = []
    for parity in range(2):
        for i in range(LOADS):
            part = pl.ds(i * per, per)
            for j, (src, dst) in enumerate(((transfer_hbm, transfer_ref), (adjoint_hbm, adjoint_ref))):
                copy = pltpu.make_async_copy(src.at[part, parity], dst.at[parity, part], load_sems.at[j, parity, i])
                copy.start()
                loads.append(copy)
    stores = []
    for parity in range(2):
        for k in range(KL // 2):
            if k % per == 0:
                first = 2 * (parity * LOADS + k // per)
                loads[first].wait()
                loads[first + 1].wait()
            left = transfer_ref[parity, k].reshape(2 * SL, M)
            right = jnp.concatenate([adjoint_ref[parity, k, 0], adjoint_ref[parity, k, 1]], axis=1)
            full = jnp.dot(left, right, preferred_element_type=jnp.float32)
            row = parity * KL + k
            rows_ref[pl.ds(row, SL, stride=PITCH), :] = full[:SL, :C] - full[SL:, C:]
            rows_ref[pl.ds(row + KL // 2, SL, stride=PITCH), :] = full[:SL, C:] + full[SL:, :C]
        for s in range(SL):
            out_ref[s, parity] = rows_ref[pl.ds(s * PITCH + parity * KL, KL), :].astype(jnp.bfloat16)
        copy = pltpu.make_async_copy(out_ref.at[:, parity], out_hbm.at[:, parity], out_sems.at[parity])
        copy.start()
        stores.append(copy)
    for copy in stores:
        copy.wait()


def spectra_rows(transfer, adjoint):
    return pl.pallas_call(
        spectra_kernel,
        in_specs=[pl.BlockSpec(memory_space=pl.ANY)] * 2,
        out_specs=pl.BlockSpec(memory_space=pl.ANY),
        out_shape=jax.ShapeDtypeStruct((SL, 2, KL, C), jnp.bfloat16),
        scratch_shapes=[
            pltpu.VMEM((2, KL // 2, 2, SL, M), jnp.bfloat16),
            pltpu.VMEM((2, KL // 2, 2, M, C), jnp.bfloat16),
            pltpu.VMEM((SL * PITCH + PITCH + 7, C), jnp.float32),
            pltpu.VMEM((SL, 2, KL, C), jnp.bfloat16),
            pltpu.SemaphoreType.DMA((2, 2, LOADS)),
            pltpu.SemaphoreType.DMA((2,)),
        ],
        compiler_params=pltpu.CompilerParams(vmem_limit_bytes=60 * 2**20),
        name="spectra",
    )(transfer.reshape(KL // 2, 2, 2, SL, M), adjoint.reshape(KL // 2, 2, 2, M, C))


def update_kernel(lower_ref, pivots_ref, high_ref, low_ref):
    update = lax.dot_general(
        lower_ref[...], pivots_ref[...], (((1,), (1,)), ((), ())), preferred_element_type=jnp.float32
    )
    high = update.astype(jnp.bfloat16)
    high_ref[...] = high
    low_ref[...] = (update - high.astype(jnp.float32)).astype(low_ref.dtype)


def update_rows(lower, pivots):
    rows = lower.shape[0]
    return pl.pallas_call(
        update_kernel,
        in_specs=[pl.BlockSpec(memory_space=pltpu.VMEM)] * 2,
        out_specs=[pl.BlockSpec(memory_space=pltpu.VMEM)] * 2,
        out_shape=[
            jax.ShapeDtypeStruct((rows, C), jnp.bfloat16),
            jax.ShapeDtypeStruct((rows, C), jnp.float8_e5m2),
        ],
        compiler_params=pltpu.CompilerParams(vmem_limit_bytes=24 * 2**20),
        cost_estimate=pl.CostEstimate(
            flops=2 * rows * PANELS * C * C, bytes_accessed=rows * (PANELS * C * 2 + C * 3), transcendentals=0
        ),
        name="update",
    )(lower, pivots)


def panel_kernel(
    table_ref, recv_ref, high_ref, low_ref, inverse_hbm, out_hbm, out_ref, inverse_ref, block_ref, sems, sem
):
    load = pltpu.make_async_copy(inverse_hbm, inverse_ref, sem)
    load.start()
    block_ref[...] = jnp.zeros_like(block_ref)
    sides = []
    for parity in range(2):
        cols = [recv_ref[:, s, parity].reshape(NF, C) for s in range(SD)]
        sides.append(jnp.concatenate(cols, axis=1))
    stores = []
    for first in range(0, HALF, T_STEP):
        rows = table_ref[pl.ds(0, T_STEP)]
        if first > 0:
            column = lax.broadcasted_iota(jnp.int32, rows.shape, 1)
            rows = jnp.where(column % 2 == 0, rows.astype(jnp.float32), -rows.astype(jnp.float32)).astype(jnp.bfloat16)
        even = jnp.dot(rows, sides[0], preferred_element_type=jnp.float32)
        rows = table_ref[pl.ds(T_STEP + first, T_STEP)]
        odd = jnp.dot(rows, sides[1], preferred_element_type=jnp.float32)
        if first == 0:
            load.wait()
            block_ref[:C, :C] = inverse_ref[...]
            block_ref[C:, C:] = inverse_ref[...]
            block = block_ref[...]
        for i in range(0, T_STEP, T_CHUNK):
            chunk = slice(i, i + T_CHUNK)
            for half, sums in enumerate((even[chunk] + odd[chunk], even[chunk] - odd[chunk])):
                where = pl.ds(half * HALF + first + i, T_CHUNK)
                for s in range(0, SD, 2):
                    update = [
                        high_ref[j, where].astype(jnp.float32) + low_ref[j, where].astype(jnp.float32)
                        for j in (s, s + 1)
                    ]
                    update = jnp.concatenate(update, axis=1)
                    reduced = (sums[:, s * C : (s + 2) * C] - update).astype(jnp.bfloat16)
                    both = jnp.dot(reduced, block, preferred_element_type=jnp.float32).astype(jnp.bfloat16)
                    out_ref[s, where] = both[:, :C]
                    out_ref[s + 1, where] = both[:, C:]
                copy = pltpu.make_async_copy(out_ref.at[:, where], out_hbm.at[:, where], sems.at[len(stores)])
                copy.start()
                stores.append(copy)
    for copy in stores:
        copy.wait()


def panel_rows(table, recv, high, low, inverse):
    return pl.pallas_call(
        panel_kernel,
        in_specs=[pl.BlockSpec(memory_space=pltpu.VMEM)] * 4 + [pl.BlockSpec(memory_space=pl.ANY)],
        out_specs=pl.BlockSpec(memory_space=pl.ANY),
        out_shape=jax.ShapeDtypeStruct((SD, NT, C), jnp.bfloat16),
        scratch_shapes=[
            pltpu.VMEM((SD, NT, C), jnp.bfloat16),
            pltpu.VMEM((C, C), jnp.bfloat16),
            pltpu.VMEM((2 * C, 2 * C), jnp.bfloat16),
            pltpu.SemaphoreType.DMA((NT // T_CHUNK,)),
            pltpu.SemaphoreType.DMA,
        ],
        compiler_params=pltpu.CompilerParams(vmem_limit_bytes=24 * 2**20),
        name="panel",
    )(table, recv, high, low, inverse)


def gather_pivots(pivot_store, owners):
    mine = jnp.repeat(owners == lax.axis_index("grp"), C)[None, :]
    value = jnp.where(mine, pivot_store, jnp.zeros_like(pivot_store))
    for bit in (1, 2, 4):
        value = value + lax.ppermute(value, "grp", [(g, g ^ bit) for g in range(N_GRP)])
    return value


def per_device(transfer, adjoint, lower_rows, pivot_store, owners, inverse_factor):
    rows = spectra_rows(transfer, adjoint)
    recv = lax.all_to_all(rows.reshape(N_FREQ, SD, 2, KL, C), "freq", split_axis=0, concat_axis=0, tiled=True)
    pivots = gather_pivots(pivot_store, owners)
    high, low = update_rows(lower_rows, pivots)
    out = panel_rows(jnp.asarray(table_parts()), recv, high.reshape(SD, NT, C), low.reshape(SD, NT, C), inverse_factor)
    return out.reshape(SD * NT, C)


def solution(mesh):
    in_specs = (
        P("freq", None, "grp", None),
        P("freq", None, None, None),
        P(("grp", "freq"), None),
        P("grp", None),
        P(),
        P(),
    )
    out_specs = P(("grp", "freq"), None)
    return jax.shard_map(
        per_device, mesh=mesh, in_specs=in_specs, out_specs=out_specs, check_vma=False
    )
```

time: 47.5 us -> 46 us (0.968)
  local copies, waits for them, and re-layouts: 3.2 us -> 1.98 us
  Pallas kernels: 8.76 us -> 7.88 us
  waiting for transfers between devices: 19 us -> 19.5 us
    unnamed x10, local copies, waits for them, and re-layouts: 3.12 us -> 1.91 us
    all_to_all x1, waiting for transfers between devices: 6.5 us -> 7 us  [per_device(): lax.all_to_all(rows.reshape(N_FREQ, SD, 2, KL, C), 'freq', split_axis=0,...]
    pallas_call x1, Pallas kernels: 1.48 us -> 0.99 us  [update_rows(): pl.pallas_call(update_kernel, in_specs=[pl.BlockSpec(memory_space=pltpu.V...]
  transfers between devices with their start and end apart: 4 -> 4, of which waited for: 4 -> 4; matrix products, arithmetic and copies ran while one was open for 0% -> 0% of each run, Pallas kernels for 3% -> 2%
where the time goes in v3:
time: 46 us; the launch traced here: 45.2 us
  waiting for transfers between devices  19.5 us (42%)
  starting transfers between devices  15.7 us (34%)
  Pallas kernels  7.88 us (17%)
  local copies, waits for them, and re-layouts  1.98 us (4%)
    ppermute x3, waiting for transfers between devices, gather_pivots(): lax.ppermute(value, 'grp', [(g, g ^ bit) for g in range(N_GRP)])  12.5 us
    all_to_all x1, starting transfers between devices, per_device(): lax.all_to_all(rows.reshape(N_FREQ, SD, 2, KL, C), 'freq', split_axis=0,...  9.93 us
    all_to_all x1, waiting for transfers between devices, per_device(): lax.all_to_all(rows.reshape(N_FREQ, SD, 2, KL, C), 'freq', split_axis=0,...  7 us
    ppermute x3, starting transfers between devices, gather_pivots(): lax.ppermute(value, 'grp', [(g, g ^ bit) for g in range(N_GRP)])  5.73 us
    pallas_call x1, Pallas kernels, spectra_rows(): pl.pallas_call(spectra_kernel, in_specs=[pl.BlockSpec(memory_space=pl.ANY...  4.75 us
    pallas_call x1, Pallas kernels, panel_rows(): pl.pallas_call(panel_kernel, in_specs=[pl.BlockSpec(memory_space=pltpu.VM...  2.14 us
    unnamed x10, local copies, waits for them, and re-layouts  1.91 us
    pallas_call x1, Pallas kernels, update_rows(): pl.pallas_call(update_kernel, in_specs=[pl.BlockSpec(memory_space=pltpu.V...  0.99 us
  transfers between devices with their start and end apart: 4, of which 4 were waited for; matrix products, arithmetic and copies ran while one was open for 0% of the time, Pallas kernels for 2%

profile of v3, /device:TPU:8, one launch (start us, length us, event | category | flops | bytes accessed | tf_op | source)
XLA Modules:
  0.0 45.2 jit_solution(17211612908982850208)
XLA Ops:
  0.0 0.0 copy-start.4
  0.0 0.0 copy-start.3
  0.0 4.8 %spectra.1 = bf16[128,2,16,128]{3,2,1,0:T(8,128)(2,1)} custom-call(bf16[8,2,2,128,512]{4,3,2,1,0:T(8,128)(2,1)} %bitcast.11, bf16[8,2,2,512,128]{4,3,2,1,0:T(8,128)(2,1)} %bitcast.12), custom_call_target="tpu_custom_call" | custom-call | tf_op jit(solution)/shard_map/spectra/pallas_call | solution.py:72
  4.8 0.0 copy-start.1
  4.8 0.0 copy-start.2
  4.8 9.9 %all-to-all-start = ((bf16[32,4,2,16,128]{4,3,2,1,0:T(8,128)(2,1)}), bf16[32,4,2,16,128]{4,3,2,1,0:T(8,128)(2,1)S(1)}, u32[]{:S(2)}, u32[]{:S(2)}) async-start(bf16[32,4,2,16,128]{4,3,2,1,0:T(8,128)(2,1)} %bitcast.10), calls=%async_computation | async-start | bytes 2097152 | tf_op jit(solution)/shard_map/all_to_all | solution.py:190
  14.7 0.0 copy-done.4
  14.7 0.1 broadcast_bitcast_fusion
  14.8 0.0 copy-done.3
  14.8 0.5 %collective-permute-start = (bf16[128,384]{1,0:T(8,128)(2,1)S(1)}, bf16[128,384]{1,0:T(8,128)(2,1)S(1)}, u32[]{:S(2)}, u32[]{:S(2)}) collective-permute-start(bf16[128,384]{1,0:T(8,128)(2,1)S(1)} %broadcast_select_fusion), channel_id=1, source_target_pairs={{0,32},{32,0},{64,96},{96,64},{128,160},{160,128},{192,224},{224,1... | collective-permute-start | bytes 294920 | tf_op jit(solution)/shard_map/ppermute | solution.py:184
  15.4 4.5 %collective-permute-done = bf16[128,384]{1,0:T(8,128)(2,1)S(1)} collective-permute-done((bf16[128,384]{1,0:T(8,128)(2,1)S(1)}, bf16[128,384]{1,0:T(8,128)(2,1)S(1)}, u32[]{:S(2)}, u32[]{:S(2)}) %collective-permute-start) | collective-permute-done | bytes 98336 | tf_op jit(solution)/shard_map/ppermute | solution.py:184
  19.9 2.4 %collective-permute-start.1 = (bf16[128,384]{1,0:T(8,128)(2,1)S(1)}, bf16[128,384]{1,0:T(8,128)(2,1)S(1)}, u32[]{:S(2)}, u32[]{:S(2)}) collective-permute-start(bf16[128,384]{1,0:T(8,128)(2,1)S(1)} %fusion), channel_id=1, source_target_pairs={{0,64},{32,96},{64,0},{96,32},{128,192},{160,224},{192,128},{224,1... | collective-permute-start | bytes 294920 | tf_op jit(solution)/shard_map/ppermute | solution.py:184
  22.3 3.8 %collective-permute-done.1 = bf16[128,384]{1,0:T(8,128)(2,1)S(1)} collective-permute-done((bf16[128,384]{1,0:T(8,128)(2,1)S(1)}, bf16[128,384]{1,0:T(8,128)(2,1)S(1)}, u32[]{:S(2)}, u32[]{:S(2)}) %collective-permute-start.1) | collective-permute-done | bytes 98336 | tf_op jit(solution)/shard_map/ppermute | solution.py:184
  26.2 2.8 %collective-permute-start.2 = (bf16[128,384]{1,0:T(8,128)(2,1)S(1)}, bf16[128,384]{1,0:T(8,128)(2,1)S(1)}, u32[]{:S(2)}, u32[]{:S(2)}) collective-permute-start(bf16[128,384]{1,0:T(8,128)(2,1)S(1)} %add.10), channel_id=1, source_target_pairs={{0,128},{32,160},{64,192},{96,224},{128,0},{160,32},{192,64},{224,... | collective-permute-start | bytes 294920 | tf_op jit(solution)/shard_map/ppermute | solution.py:184
  29.0 4.2 %collective-permute-done.2 = bf16[128,384]{1,0:T(8,128)(2,1)S(1)} collective-permute-done((bf16[128,384]{1,0:T(8,128)(2,1)S(1)}, bf16[128,384]{1,0:T(8,128)(2,1)S(1)}, u32[]{:S(2)}, u32[]{:S(2)}) %collective-permute-start.2) | collective-permute-done | bytes 98336 | tf_op jit(solution)/shard_map/ppermute | solution.py:184
  33.2 0.0 copy-start
  33.2 1.9 %copy-done = bf16[4096,384]{1,0:T(8,128)(2,1)S(1)} copy-done((bf16[4096,384]{1,0:T(8,128)(2,1)S(1)}, bf16[4096,384]{1,0:T(8,128)(2,1)}, u32[]{:S(2)}) %copy-start) | copy-done | bytes 3145752
  35.1 1.0 %update.1 = (bf16[4096,128]{1,0:T(8,128)(2,1)S(1)}, f8e5m2[4096,128]{1,0:T(32,128)(4,1)S(1)}) custom-call(bf16[4096,384]{1,0:T(8,128)(2,1)S(1)} %copy-done, bf16[128,384]{1,0:T(8,128)(2,1)S(1)} %add.11.pivots_ref), custom_call_target="tpu_custom_call" | custom-call | flops 402653184 | bytes 4718592 | tf_op jit(solution)/shard_map/update/pallas_call | solution.py:101
  36.1 7.0 %all-to-all-done.recv_ref = bf16[32,4,2,16,128]{4,3,2,1,0:T(8,128)(2,1)S(1)} async-done(((bf16[32,4,2,16,128]{4,3,2,1,0:T(8,128)(2,1)}), bf16[32,4,2,16,128]{4,3,2,1,0:T(8,128)(2,1)S(1)}, u32[]{:S(2)}, u32[]{:S(2)}) %all-to-all-start) | async-done | bytes 1048608 | tf_op jit(solution)/shard_map/all_to_all | solution.py:190
  43.1 0.0 copy-done.1
  43.1 0.0 copy-done.2
  43.1 2.1 %panel.1 = bf16[4,1024,128]{2,1,0:T(8,128)(2,1)} custom-call(bf16[768,512]{1,0:T(8,128)(2,1)S(1)} %copy-done.1, bf16[32,4,2,16,128]{4,3,2,1,0:T(8,128)(2,1)S(1)} %all-to-all-done.recv_ref, bf16[4,1024,128]{2,1,0:T(8,128)(2,1)S(1)} %bitcast.8, f8e5m2[4,1024,128]{2,1,0:T(32,128)(4,1)S(1)} %bitcast.9, bf16[128,128]{1,0:T(8,128)(2,1)S(1)} %copy-done.2), custom_call_target="tpu_custom_call" | custom-call | tf_op jit(solution)/shard_map/panel/pallas_call | solution.py:163
  (5 shorter events, 0.1 us)
Async XLA Ops:
  0.0 14.7 %copy-start.4 = (s32[3]{0:T(128)S(1)}, s32[3]{0:T(128)}, u32[]{:S(2)}) copy-start(s32[3]{0:T(128)} %param.11) | copy-start | bytes 40
  0.0 14.8 %copy-start.3 = (bf16[128,384]{1,0:T(8,128)(2,1)S(1)}, bf16[128,384]{1,0:T(8,128)(2,1)}, u32[]{:S(2)}) copy-start(bf16[128,384]{1,0:T(8,128)(2,1)} %param.10) | copy-start | bytes 294916
  4.8 38.3 %copy-start.1 = (bf16[768,512]{1,0:T(8,128)(2,1)S(1)}, bf16[768,512]{1,0:T(8,128)(2,1)}, u32[]{:S(2)}) copy-start(bf16[768,512]{1,0:T(8,128)(2,1)} %constant.10.clone.table_ref) | copy-start | bytes 2359300
  4.8 38.3 %copy-start.2 = (bf16[128,128]{1,0:T(8,128)(2,1)S(1)}, bf16[128,128]{1,0:T(8,128)(2,1)}, u32[]{:S(2)}) copy-start(bf16[128,128]{1,0:T(8,128)(2,1)} %inverse_hbm.1) | copy-start | bytes 98308
  4.8 38.3 %all-to-all-start = ((bf16[32,4,2,16,128]{4,3,2,1,0:T(8,128)(2,1)}), bf16[32,4,2,16,128]{4,3,2,1,0:T(8,128)(2,1)S(1)}, u32[]{:S(2)}, u32[]{:S(2)}) async-start(bf16[32,4,2,16,128]{4,3,2,1,0:T(8,128)(2,1)} %bitcast.10), calls=%async_computation | async-start | bytes 2097152 | tf_op jit(solution)/shard_map/all_to_all | solution.py:190
  14.8 5.1 %collective-permute-start = (bf16[128,384]{1,0:T(8,128)(2,1)S(1)}, bf16[128,384]{1,0:T(8,128)(2,1)S(1)}, u32[]{:S(2)}, u32[]{:S(2)}) collective-permute-start(bf16[128,384]{1,0:T(8,128)(2,1)S(1)} %broadcast_select_fusion), channel_id=1, source_target_pairs={{0,32},{32,0},{64,96},{96,64},{128,160},{160,128},{192,224},{224,1... | collective-permute-start | bytes 294920 | tf_op jit(solution)/shard_map/ppermute | solution.py:184
  19.9 6.2 %collective-permute-start.1 = (bf16[128,384]{1,0:T(8,128)(2,1)S(1)}, bf16[128,384]{1,0:T(8,128)(2,1)S(1)}, u32[]{:S(2)}, u32[]{:S(2)}) collective-permute-start(bf16[128,384]{1,0:T(8,128)(2,1)S(1)} %fusion), channel_id=1, source_target_pairs={{0,64},{32,96},{64,0},{96,32},{128,192},{160,224},{192,128},{224,1... | collective-permute-start | bytes 294920 | tf_op jit(solution)/shard_map/ppermute | solution.py:184
  26.2 7.0 %collective-permute-start.2 = (bf16[128,384]{1,0:T(8,128)(2,1)S(1)}, bf16[128,384]{1,0:T(8,128)(2,1)S(1)}, u32[]{:S(2)}, u32[]{:S(2)}) collective-permute-start(bf16[128,384]{1,0:T(8,128)(2,1)S(1)} %add.10), channel_id=1, source_target_pairs={{0,128},{32,160},{64,192},{96,224},{128,0},{160,32},{192,64},{224,... | collective-permute-start | bytes 294920 | tf_op jit(solution)/shard_map/ppermute | solution.py:184
  33.2 1.9 %copy-start = (bf16[4096,384]{1,0:T(8,128)(2,1)S(1)}, bf16[4096,384]{1,0:T(8,128)(2,1)}, u32[]{:S(2)}) copy-start(bf16[4096,384]{1,0:T(8,128)(2,1)} %lower_ref.1) | copy-start | bytes 9437188

commit v4 on v3

--- a/solution.py
+++ b/solution.py
@@ -19,6 +19,7 @@
 KL = NF // N_FREQ
 SL = NS // N_GRP
 SD = SL // N_FREQ
+ORDER = [x * 16 + (z + 5) % 8 * 2 + core for x in range(2) for z in range(8) for core in range(2)]
 ROWS = 2 * KL
 PITCH = ROWS + 1
 LOADS = 4
@@ -30,7 +31,7 @@
 def table_parts():
     phases = np.arange(HALF)[:, None] * np.arange(NF)[None, :] % NT * (2.0 * math.pi / NT)
     table = np.stack([np.cos(phases), -np.sin(phases)], axis=1) / math.sqrt(NF)
-    table = table.reshape(HALF, 2, N_FREQ, KL // 2, 2).transpose(4, 0, 2, 1, 3).reshape(2, HALF, NF)
+    table = table.reshape(HALF, 2, N_FREQ, KL // 2, 2)[:, :, ORDER].transpose(4, 0, 2, 1, 3).reshape(2, HALF, NF)
     return np.concatenate([table[0, : HALF // 2], table[1]]).astype(jnp.bfloat16)
 
 
@@ -60,7 +61,8 @@
             rows_ref[pl.ds(row, SL, stride=PITCH), :] = full[:SL, :C] - full[SL:, C:]
             rows_ref[pl.ds(row + KL // 2, SL, stride=PITCH), :] = full[:SL, C:] + full[SL:, :C]
         for s in range(SL):
-            out_ref[s, parity] = rows_ref[pl.ds(s * PITCH + parity * KL, KL), :].astype(jnp.bfloat16)
+            place = ORDER.index(s // SD) * SD + s % SD
+            out_ref[place, parity] = rows_ref[pl.ds(s * PITCH + parity * KL, KL), :].astype(jnp.bfloat16)
         copy = pltpu.make_async_copy(out_ref.at[:, parity], out_hbm.at[:, parity], out_sems.at[parity])
         copy.start()
         stores.append(copy)
@@ -187,7 +189,8 @@
 
 def per_device(transfer, adjoint, lower_rows, pivot_store, owners, inverse_factor):
     rows = spectra_rows(transfer, adjoint)
-    recv = lax.all_to_all(rows.reshape(N_FREQ, SD, 2, KL, C), "freq", split_axis=0, concat_axis=0, tiled=True)
+    rows = rows.reshape(N_FREQ, SD, 2, KL, C)
+    recv = lax.all_to_all(rows, "freq", split_axis=0, concat_axis=0, axis_index_groups=[ORDER], tiled=True)
     pivots = gather_pivots(pivot_store, owners)
     high, low = update_rows(lower_rows, pivots)
     out = panel_rows(jnp.asarray(table_parts()), recv, high.reshape(SD, NT, C), low.reshape(SD, NT, C), inverse_factor)

time: 46 us -> 43.1 us (0.937)
  the two profiles are of different devices: /device:TPU:8 before, /device:TPU:1 now
where the time goes in v4:
time: 43.1 us; the launch traced here: 42.9 us
  starting transfers between devices  18.9 us (44%)
  waiting for transfers between devices  14 us (32%)
  Pallas kernels  7.87 us (18%)
  local copies, waits for them, and re-layouts  1.98 us (5%)
    all_to_all x1, starting transfers between devices, per_device(): lax.all_to_all(rows, 'freq', split_axis=0, concat_axis=0, axis_index_grou...  11.9 us
    ppermute x3, waiting for transfers between devices, gather_pivots(): lax.ppermute(value, 'grp', [(g, g ^ bit) for g in range(N_GRP)])  8.9 us
    ppermute x3, starting transfers between devices, gather_pivots(): lax.ppermute(value, 'grp', [(g, g ^ bit) for g in range(N_GRP)])  7 us
    all_to_all x1, waiting for transfers between devices, per_device(): lax.all_to_all(rows, 'freq', split_axis=0, concat_axis=0, axis_index_grou...  5.06 us
    pallas_call x1, Pallas kernels, spectra_rows(): pl.pallas_call(spectra_kernel, in_specs=[pl.BlockSpec(memory_space=pl.ANY...  4.75 us
    pallas_call x1, Pallas kernels, panel_rows(): pl.pallas_call(panel_kernel, in_specs=[pl.BlockSpec(memory_space=pltpu.VM...  2.14 us
    unnamed x10, local copies, waits for them, and re-layouts  1.91 us
    pallas_call x1, Pallas kernels, update_rows(): pl.pallas_call(update_kernel, in_specs=[pl.BlockSpec(memory_space=pltpu.V...  0.98 us
  transfers between devices with their start and end apart: 4, of which 4 were waited for; matrix products, arithmetic and copies ran while one was open for 0% of the time, Pallas kernels for 2%

profile of v4, /device:TPU:1, one launch (start us, length us, event | category | flops | bytes accessed | tf_op | source)
XLA Modules:
  0.0 42.9 jit_solution(2208235825307550487)
XLA Ops:
  0.0 0.0 copy-start.4
  0.0 0.0 copy-start.3
  0.0 4.7 %spectra.1 = bf16[128,2,16,128]{3,2,1,0:T(8,128)(2,1)} custom-call(bf16[8,2,2,128,512]{4,3,2,1,0:T(8,128)(2,1)} %bitcast.11, bf16[8,2,2,512,128]{4,3,2,1,0:T(8,128)(2,1)} %bitcast.12), custom_call_target="tpu_custom_call" | custom-call | tf_op jit(solution)/shard_map/spectra/pallas_call | solution.py:74
  4.8 0.0 copy-start.1
  4.8 0.0 copy-start.2
  4.8 11.9 %all-to-all-start = ((bf16[32,4,2,16,128]{4,3,2,1,0:T(8,128)(2,1)}), bf16[32,4,2,16,128]{4,3,2,1,0:T(8,128)(2,1)S(1)}, u32[]{:S(2)}, u32[]{:S(2)}) async-start(bf16[32,4,2,16,128]{4,3,2,1,0:T(8,128)(2,1)} %bitcast.10), calls=%async_computation | async-start | bytes 2097152 | tf_op jit(solution)/shard_map/all_to_all | solution.py:193
  16.7 0.0 copy-done.4
  16.7 0.1 broadcast_bitcast_fusion
  16.8 0.0 copy-done.3
  16.8 1.4 %collective-permute-start = (bf16[128,384]{1,0:T(8,128)(2,1)S(1)}, bf16[128,384]{1,0:T(8,128)(2,1)S(1)}, u32[]{:S(2)}, u32[]{:S(2)}) collective-permute-start(bf16[128,384]{1,0:T(8,128)(2,1)S(1)} %broadcast_select_fusion), channel_id=1, source_target_pairs={{0,32},{32,0},{64,96},{96,64},{128,160},{160,128},{192,224},{224,1... | collective-permute-start | bytes 294920 | tf_op jit(solution)/shard_map/ppermute | solution.py:186
  18.2 2.7 %collective-permute-done = bf16[128,384]{1,0:T(8,128)(2,1)S(1)} collective-permute-done((bf16[128,384]{1,0:T(8,128)(2,1)S(1)}, bf16[128,384]{1,0:T(8,128)(2,1)S(1)}, u32[]{:S(2)}, u32[]{:S(2)}) %collective-permute-start) | collective-permute-done | bytes 98336 | tf_op jit(solution)/shard_map/ppermute | solution.py:186
  20.9 3.0 %collective-permute-start.1 = (bf16[128,384]{1,0:T(8,128)(2,1)S(1)}, bf16[128,384]{1,0:T(8,128)(2,1)S(1)}, u32[]{:S(2)}, u32[]{:S(2)}) collective-permute-start(bf16[128,384]{1,0:T(8,128)(2,1)S(1)} %fusion), channel_id=1, source_target_pairs={{0,64},{32,96},{64,0},{96,32},{128,192},{160,224},{192,128},{224,1... | collective-permute-start | bytes 294920 | tf_op jit(solution)/shard_map/ppermute | solution.py:186
  23.9 2.4 %collective-permute-done.1 = bf16[128,384]{1,0:T(8,128)(2,1)S(1)} collective-permute-done((bf16[128,384]{1,0:T(8,128)(2,1)S(1)}, bf16[128,384]{1,0:T(8,128)(2,1)S(1)}, u32[]{:S(2)}, u32[]{:S(2)}) %collective-permute-start.1) | collective-permute-done | bytes 98336 | tf_op jit(solution)/shard_map/ppermute | solution.py:186
  26.3 2.6 %collective-permute-start.2 = (bf16[128,384]{1,0:T(8,128)(2,1)S(1)}, bf16[128,384]{1,0:T(8,128)(2,1)S(1)}, u32[]{:S(2)}, u32[]{:S(2)}) collective-permute-start(bf16[128,384]{1,0:T(8,128)(2,1)S(1)} %add.10), channel_id=1, source_target_pairs={{0,128},{32,160},{64,192},{96,224},{128,0},{160,32},{192,64},{224,... | collective-permute-start | bytes 294920 | tf_op jit(solution)/shard_map/ppermute | solution.py:186
  28.9 3.8 %collective-permute-done.2 = bf16[128,384]{1,0:T(8,128)(2,1)S(1)} collective-permute-done((bf16[128,384]{1,0:T(8,128)(2,1)S(1)}, bf16[128,384]{1,0:T(8,128)(2,1)S(1)}, u32[]{:S(2)}, u32[]{:S(2)}) %collective-permute-start.2) | collective-permute-done | bytes 98336 | tf_op jit(solution)/shard_map/ppermute | solution.py:186
  32.8 0.0 copy-start
  32.8 1.9 %copy-done = bf16[4096,384]{1,0:T(8,128)(2,1)S(1)} copy-done((bf16[4096,384]{1,0:T(8,128)(2,1)S(1)}, bf16[4096,384]{1,0:T(8,128)(2,1)}, u32[]{:S(2)}) %copy-start) | copy-done | bytes 3145752
  34.7 1.0 %update.1 = (bf16[4096,128]{1,0:T(8,128)(2,1)S(1)}, f8e5m2[4096,128]{1,0:T(32,128)(4,1)S(1)}) custom-call(bf16[4096,384]{1,0:T(8,128)(2,1)S(1)} %copy-done, bf16[128,384]{1,0:T(8,128)(2,1)S(1)} %add.11.pivots_ref), custom_call_target="tpu_custom_call" | custom-call | flops 402653184 | bytes 4718592 | tf_op jit(solution)/shard_map/update/pallas_call | solution.py:103
  35.6 5.1 %all-to-all-done.recv_ref = bf16[32,4,2,16,128]{4,3,2,1,0:T(8,128)(2,1)S(1)} async-done(((bf16[32,4,2,16,128]{4,3,2,1,0:T(8,128)(2,1)}), bf16[32,4,2,16,128]{4,3,2,1,0:T(8,128)(2,1)S(1)}, u32[]{:S(2)}, u32[]{:S(2)}) %all-to-all-start) | async-done | bytes 1048608 | tf_op jit(solution)/shard_map/all_to_all | solution.py:193
  40.7 0.0 copy-done.1
  40.7 0.0 copy-done.2
  40.7 2.1 %panel.1 = bf16[4,1024,128]{2,1,0:T(8,128)(2,1)} custom-call(bf16[768,512]{1,0:T(8,128)(2,1)S(1)} %copy-done.1, bf16[32,4,2,16,128]{4,3,2,1,0:T(8,128)(2,1)S(1)} %all-to-all-done.recv_ref, bf16[4,1024,128]{2,1,0:T(8,128)(2,1)S(1)} %bitcast.8, f8e5m2[4,1024,128]{2,1,0:T(32,128)(4,1)S(1)} %bitcast.9, bf16[128,128]{1,0:T(8,128)(2,1)S(1)} %copy-done.2), custom_call_target="tpu_custom_call" | custom-call | tf_op jit(solution)/shard_map/panel/pallas_call | solution.py:165
  (5 shorter events, 0.1 us)
Async XLA Ops:
  0.0 16.7 %copy-start.4 = (s32[3]{0:T(128)S(1)}, s32[3]{0:T(128)}, u32[]{:S(2)}) copy-start(s32[3]{0:T(128)} %param.11) | copy-start | bytes 40
  0.0 16.8 %copy-start.3 = (bf16[128,384]{1,0:T(8,128)(2,1)S(1)}, bf16[128,384]{1,0:T(8,128)(2,1)}, u32[]{:S(2)}) copy-start(bf16[128,384]{1,0:T(8,128)(2,1)} %param.10) | copy-start | bytes 294916
  4.8 35.9 %copy-start.1 = (bf16[768,512]{1,0:T(8,128)(2,1)S(1)}, bf16[768,512]{1,0:T(8,128)(2,1)}, u32[]{:S(2)}) copy-start(bf16[768,512]{1,0:T(8,128)(2,1)} %constant.10.clone.table_ref) | copy-start | bytes 2359300
  4.8 35.9 %copy-start.2 = (bf16[128,128]{1,0:T(8,128)(2,1)S(1)}, bf16[128,128]{1,0:T(8,128)(2,1)}, u32[]{:S(2)}) copy-start(bf16[128,128]{1,0:T(8,128)(2,1)} %inverse_hbm.1) | copy-start | bytes 98308
  4.8 35.9 %all-to-all-start = ((bf16[32,4,2,16,128]{4,3,2,1,0:T(8,128)(2,1)}), bf16[32,4,2,16,128]{4,3,2,1,0:T(8,128)(2,1)S(1)}, u32[]{:S(2)}, u32[]{:S(2)}) async-start(bf16[32,4,2,16,128]{4,3,2,1,0:T(8,128)(2,1)} %bitcast.10), calls=%async_computation | async-start | bytes 2097152 | tf_op jit(solution)/shard_map/all_to_all | solution.py:193
  16.8 4.1 %collective-permute-start = (bf16[128,384]{1,0:T(8,128)(2,1)S(1)}, bf16[128,384]{1,0:T(8,128)(2,1)S(1)}, u32[]{:S(2)}, u32[]{:S(2)}) collective-permute-start(bf16[128,384]{1,0:T(8,128)(2,1)S(1)} %broadcast_select_fusion), channel_id=1, source_target_pairs={{0,32},{32,0},{64,96},{96,64},{128,160},{160,128},{192,224},{224,1... | collective-permute-start | bytes 294920 | tf_op jit(solution)/shard_map/ppermute | solution.py:186
  20.9 5.4 %collective-permute-start.1 = (bf16[128,384]{1,0:T(8,128)(2,1)S(1)}, bf16[128,384]{1,0:T(8,128)(2,1)S(1)}, u32[]{:S(2)}, u32[]{:S(2)}) collective-permute-start(bf16[128,384]{1,0:T(8,128)(2,1)S(1)} %fusion), channel_id=1, source_target_pairs={{0,64},{32,96},{64,0},{96,32},{128,192},{160,224},{192,128},{224,1... | collective-permute-start | bytes 294920 | tf_op jit(solution)/shard_map/ppermute | solution.py:186
  26.3 6.4 %collective-permute-start.2 = (bf16[128,384]{1,0:T(8,128)(2,1)S(1)}, bf16[128,384]{1,0:T(8,128)(2,1)S(1)}, u32[]{:S(2)}, u32[]{:S(2)}) collective-permute-start(bf16[128,384]{1,0:T(8,128)(2,1)S(1)} %add.10), channel_id=1, source_target_pairs={{0,128},{32,160},{64,192},{96,224},{128,0},{160,32},{192,64},{224,... | collective-permute-start | bytes 294920 | tf_op jit(solution)/shard_map/ppermute | solution.py:186
  32.8 1.9 %copy-start = (bf16[4096,384]{1,0:T(8,128)(2,1)S(1)}, bf16[4096,384]{1,0:T(8,128)(2,1)}, u32[]{:S(2)}) copy-start(bf16[4096,384]{1,0:T(8,128)(2,1)} %lower_ref.1) | copy-start | bytes 9437188

commit v5 on v4

--- a/solution.py
+++ b/solution.py
@@ -19,7 +19,7 @@
 KL = NF // N_FREQ
 SL = NS // N_GRP
 SD = SL // N_FREQ
-ORDER = [x * 16 + (z + 5) % 8 * 2 + core for x in range(2) for z in range(8) for core in range(2)]
+ORDER = [x * 16 + (z + 5) % 8 * 2 + 1 - core for x in range(2) for z in range(8) for core in range(2)]
 ROWS = 2 * KL
 PITCH = ROWS + 1
 LOADS = 4

time: 43.1 us -> 42.6 us (0.988)
  the two profiles are of different devices: /device:TPU:1 before, /device:TPU:8 now
where the time goes in v5:
time: 42.6 us; the launch traced here: 41.9 us
  starting transfers between devices  16.2 us (38%)
  waiting for transfers between devices  15.7 us (37%)
  Pallas kernels  7.88 us (18%)
  local copies, waits for them, and re-layouts  1.98 us (5%)
    ppermute x3, waiting for transfers between devices, gather_pivots(): lax.ppermute(value, 'grp', [(g, g ^ bit) for g in range(N_GRP)])  12.7 us
    all_to_all x1, starting transfers between devices, per_device(): lax.all_to_all(rows, 'freq', split_axis=0, concat_axis=0, axis_index_grou...  10.5 us
    ppermute x3, starting transfers between devices, gather_pivots(): lax.ppermute(value, 'grp', [(g, g ^ bit) for g in range(N_GRP)])  5.73 us
    pallas_call x1, Pallas kernels, spectra_rows(): pl.pallas_call(spectra_kernel, in_specs=[pl.BlockSpec(memory_space=pl.ANY...  4.75 us
    all_to_all x1, waiting for transfers between devices, per_device(): lax.all_to_all(rows, 'freq', split_axis=0, concat_axis=0, axis_index_grou...  2.99 us
    pallas_call x1, Pallas kernels, panel_rows(): pl.pallas_call(panel_kernel, in_specs=[pl.BlockSpec(memory_space=pltpu.VM...  2.14 us
    unnamed x10, local copies, waits for them, and re-layouts  1.91 us
    pallas_call x1, Pallas kernels, update_rows(): pl.pallas_call(update_kernel, in_specs=[pl.BlockSpec(memory_space=pltpu.V...  0.99 us
  transfers between devices with their start and end apart: 4, of which 4 were waited for; matrix products, arithmetic and copies ran while one was open for 0% of the time, Pallas kernels for 2%

profile of v5, /device:TPU:8, one launch (start us, length us, event | category | flops | bytes accessed | tf_op | source)
XLA Modules:
  0.0 41.9 jit_solution(9723507952423156191)
XLA Ops:
  0.0 0.0 copy-start.4
  0.0 0.0 copy-start.3
  0.0 4.8 %spectra.1 = bf16[128,2,16,128]{3,2,1,0:T(8,128)(2,1)} custom-call(bf16[8,2,2,128,512]{4,3,2,1,0:T(8,128)(2,1)} %bitcast.11, bf16[8,2,2,512,128]{4,3,2,1,0:T(8,128)(2,1)} %bitcast.12), custom_call_target="tpu_custom_call" | custom-call | tf_op jit(solution)/shard_map/spectra/pallas_call | solution.py:74
  4.8 0.0 copy-start.1
  4.8 0.0 copy-start.2
  4.8 10.5 %all-to-all-start = ((bf16[32,4,2,16,128]{4,3,2,1,0:T(8,128)(2,1)}), bf16[32,4,2,16,128]{4,3,2,1,0:T(8,128)(2,1)S(1)}, u32[]{:S(2)}, u32[]{:S(2)}) async-start(bf16[32,4,2,16,128]{4,3,2,1,0:T(8,128)(2,1)} %bitcast.10), calls=%async_computation | async-start | bytes 2097152 | tf_op jit(solution)/shard_map/all_to_all | solution.py:193
  15.3 0.0 copy-done.4
  15.3 0.1 broadcast_bitcast_fusion
  15.4 0.0 copy-done.3
  15.4 0.5 %collective-permute-start = (bf16[128,384]{1,0:T(8,128)(2,1)S(1)}, bf16[128,384]{1,0:T(8,128)(2,1)S(1)}, u32[]{:S(2)}, u32[]{:S(2)}) collective-permute-start(bf16[128,384]{1,0:T(8,128)(2,1)S(1)} %broadcast_select_fusion), channel_id=1, source_target_pairs={{0,32},{32,0},{64,96},{96,64},{128,160},{160,128},{192,224},{224,1... | collective-permute-start | bytes 294920 | tf_op jit(solution)/shard_map/ppermute | solution.py:186
  15.9 4.3 %collective-permute-done = bf16[128,384]{1,0:T(8,128)(2,1)S(1)} collective-permute-done((bf16[128,384]{1,0:T(8,128)(2,1)S(1)}, bf16[128,384]{1,0:T(8,128)(2,1)S(1)}, u32[]{:S(2)}, u32[]{:S(2)}) %collective-permute-start) | collective-permute-done | bytes 98336 | tf_op jit(solution)/shard_map/ppermute | solution.py:186
  20.3 2.4 %collective-permute-start.1 = (bf16[128,384]{1,0:T(8,128)(2,1)S(1)}, bf16[128,384]{1,0:T(8,128)(2,1)S(1)}, u32[]{:S(2)}, u32[]{:S(2)}) collective-permute-start(bf16[128,384]{1,0:T(8,128)(2,1)S(1)} %fusion), channel_id=1, source_target_pairs={{0,64},{32,96},{64,0},{96,32},{128,192},{160,224},{192,128},{224,1... | collective-permute-start | bytes 294920 | tf_op jit(solution)/shard_map/ppermute | solution.py:186
  22.7 3.8 %collective-permute-done.1 = bf16[128,384]{1,0:T(8,128)(2,1)S(1)} collective-permute-done((bf16[128,384]{1,0:T(8,128)(2,1)S(1)}, bf16[128,384]{1,0:T(8,128)(2,1)S(1)}, u32[]{:S(2)}, u32[]{:S(2)}) %collective-permute-start.1) | collective-permute-done | bytes 98336 | tf_op jit(solution)/shard_map/ppermute | solution.py:186
  26.5 2.8 %collective-permute-start.2 = (bf16[128,384]{1,0:T(8,128)(2,1)S(1)}, bf16[128,384]{1,0:T(8,128)(2,1)S(1)}, u32[]{:S(2)}, u32[]{:S(2)}) collective-permute-start(bf16[128,384]{1,0:T(8,128)(2,1)S(1)} %add.10), channel_id=1, source_target_pairs={{0,128},{32,160},{64,192},{96,224},{128,0},{160,32},{192,64},{224,... | collective-permute-start | bytes 294920 | tf_op jit(solution)/shard_map/ppermute | solution.py:186
  29.3 4.5 %collective-permute-done.2 = bf16[128,384]{1,0:T(8,128)(2,1)S(1)} collective-permute-done((bf16[128,384]{1,0:T(8,128)(2,1)S(1)}, bf16[128,384]{1,0:T(8,128)(2,1)S(1)}, u32[]{:S(2)}, u32[]{:S(2)}) %collective-permute-start.2) | collective-permute-done | bytes 98336 | tf_op jit(solution)/shard_map/ppermute | solution.py:186
  33.9 0.0 copy-start
  33.9 1.9 %copy-done = bf16[4096,384]{1,0:T(8,128)(2,1)S(1)} copy-done((bf16[4096,384]{1,0:T(8,128)(2,1)S(1)}, bf16[4096,384]{1,0:T(8,128)(2,1)}, u32[]{:S(2)}) %copy-start) | copy-done | bytes 3145752
  35.8 1.0 %update.1 = (bf16[4096,128]{1,0:T(8,128)(2,1)S(1)}, f8e5m2[4096,128]{1,0:T(32,128)(4,1)S(1)}) custom-call(bf16[4096,384]{1,0:T(8,128)(2,1)S(1)} %copy-done, bf16[128,384]{1,0:T(8,128)(2,1)S(1)} %add.11.pivots_ref), custom_call_target="tpu_custom_call" | custom-call | flops 402653184 | bytes 4718592 | tf_op jit(solution)/shard_map/update/pallas_call | solution.py:103
  36.8 3.0 %all-to-all-done.recv_ref = bf16[32,4,2,16,128]{4,3,2,1,0:T(8,128)(2,1)S(1)} async-done(((bf16[32,4,2,16,128]{4,3,2,1,0:T(8,128)(2,1)}), bf16[32,4,2,16,128]{4,3,2,1,0:T(8,128)(2,1)S(1)}, u32[]{:S(2)}, u32[]{:S(2)}) %all-to-all-start) | async-done | bytes 1048608 | tf_op jit(solution)/shard_map/all_to_all | solution.py:193
  39.8 0.0 copy-done.1
  39.8 0.0 copy-done.2
  39.8 2.1 %panel.1 = bf16[4,1024,128]{2,1,0:T(8,128)(2,1)} custom-call(bf16[768,512]{1,0:T(8,128)(2,1)S(1)} %copy-done.1, bf16[32,4,2,16,128]{4,3,2,1,0:T(8,128)(2,1)S(1)} %all-to-all-done.recv_ref, bf16[4,1024,128]{2,1,0:T(8,128)(2,1)S(1)} %bitcast.8, f8e5m2[4,1024,128]{2,1,0:T(32,128)(4,1)S(1)} %bitcast.9, bf16[128,128]{1,0:T(8,128)(2,1)S(1)} %copy-done.2), custom_call_target="tpu_custom_call" | custom-call | tf_op jit(solution)/shard_map/panel/pallas_call | solution.py:165
  (5 shorter events, 0.1 us)
Async XLA Ops:
  0.0 15.3 %copy-start.4 = (s32[3]{0:T(128)S(1)}, s32[3]{0:T(128)}, u32[]{:S(2)}) copy-start(s32[3]{0:T(128)} %param.11) | copy-start | bytes 40
  0.0 15.4 %copy-start.3 = (bf16[128,384]{1,0:T(8,128)(2,1)S(1)}, bf16[128,384]{1,0:T(8,128)(2,1)}, u32[]{:S(2)}) copy-start(bf16[128,384]{1,0:T(8,128)(2,1)} %param.10) | copy-start | bytes 294916
  4.8 35.0 %copy-start.1 = (bf16[768,512]{1,0:T(8,128)(2,1)S(1)}, bf16[768,512]{1,0:T(8,128)(2,1)}, u32[]{:S(2)}) copy-start(bf16[768,512]{1,0:T(8,128)(2,1)} %constant.10.clone.table_ref) | copy-start | bytes 2359300
  4.8 35.0 %copy-start.2 = (bf16[128,128]{1,0:T(8,128)(2,1)S(1)}, bf16[128,128]{1,0:T(8,128)(2,1)}, u32[]{:S(2)}) copy-start(bf16[128,128]{1,0:T(8,128)(2,1)} %inverse_hbm.1) | copy-start | bytes 98308
  4.8 35.0 %all-to-all-start = ((bf16[32,4,2,16,128]{4,3,2,1,0:T(8,128)(2,1)}), bf16[32,4,2,16,128]{4,3,2,1,0:T(8,128)(2,1)S(1)}, u32[]{:S(2)}, u32[]{:S(2)}) async-start(bf16[32,4,2,16,128]{4,3,2,1,0:T(8,128)(2,1)} %bitcast.10), calls=%async_computation | async-start | bytes 2097152 | tf_op jit(solution)/shard_map/all_to_all | solution.py:193
  15.4 4.9 %collective-permute-start = (bf16[128,384]{1,0:T(8,128)(2,1)S(1)}, bf16[128,384]{1,0:T(8,128)(2,1)S(1)}, u32[]{:S(2)}, u32[]{:S(2)}) collective-permute-start(bf16[128,384]{1,0:T(8,128)(2,1)S(1)} %broadcast_select_fusion), channel_id=1, source_target_pairs={{0,32},{32,0},{64,96},{96,64},{128,160},{160,128},{192,224},{224,1... | collective-permute-start | bytes 294920 | tf_op jit(solution)/shard_map/ppermute | solution.py:186
  20.3 6.2 %collective-permute-start.1 = (bf16[128,384]{1,0:T(8,128)(2,1)S(1)}, bf16[128,384]{1,0:T(8,128)(2,1)S(1)}, u32[]{:S(2)}, u32[]{:S(2)}) collective-permute-start(bf16[128,384]{1,0:T(8,128)(2,1)S(1)} %fusion), channel_id=1, source_target_pairs={{0,64},{32,96},{64,0},{96,32},{128,192},{160,224},{192,128},{224,1... | collective-permute-start | bytes 294920 | tf_op jit(solution)/shard_map/ppermute | solution.py:186
  26.5 7.3 %collective-permute-start.2 = (bf16[128,384]{1,0:T(8,128)(2,1)S(1)}, bf16[128,384]{1,0:T(8,128)(2,1)S(1)}, u32[]{:S(2)}, u32[]{:S(2)}) collective-permute-start(bf16[128,384]{1,0:T(8,128)(2,1)S(1)} %add.10), channel_id=1, source_target_pairs={{0,128},{32,160},{64,192},{96,224},{128,0},{160,32},{192,64},{224,... | collective-permute-start | bytes 294920 | tf_op jit(solution)/shard_map/ppermute | solution.py:186
  33.9 1.9 %copy-start = (bf16[4096,384]{1,0:T(8,128)(2,1)S(1)}, bf16[4096,384]{1,0:T(8,128)(2,1)}, u32[]{:S(2)}) copy-start(bf16[4096,384]{1,0:T(8,128)(2,1)} %lower_ref.1) | copy-start | bytes 9437188

commit v6 on v5

--- a/solution.py
+++ b/solution.py
@@ -19,7 +19,7 @@
 KL = NF // N_FREQ
 SL = NS // N_GRP
 SD = SL // N_FREQ
-ORDER = [x * 16 + (z + 5) % 8 * 2 + 1 - core for x in range(2) for z in range(8) for core in range(2)]
+ORDER = [x * 16 + (z + 5 - x) % 8 * 2 + 1 - core for x in range(2) for z in range(8) for core in range(2)]
 ROWS = 2 * KL
 PITCH = ROWS + 1
 LOADS = 4

time: 42.6 us -> 43.6 us (1.023); the launches traced: 41.9 us -> 43.4 us
  waiting for transfers between devices: 15.7 us -> 17.1 us
    ppermute x3, waiting for transfers between devices: 12.7 us -> 13.6 us  [gather_pivots(): lax.ppermute(value, 'grp', [(g, g ^ bit) for g in range(N_GRP)])]
    all_to_all x1, waiting for transfers between devices: 2.99 us -> 3.49 us  [per_device(): lax.all_to_all(rows, 'freq', split_axis=0, concat_axis=0, axis_index_grou...]
where the time goes in v6:
time: 43.6 us; the launch traced here: 43.4 us
  waiting for transfers between devices  17.1 us (39%)
  starting transfers between devices  16.2 us (37%)
  Pallas kernels  7.87 us (18%)
  local copies, waits for them, and re-layouts  1.98 us (5%)
    ppermute x3, waiting for transfers between devices, gather_pivots(): lax.ppermute(value, 'grp', [(g, g ^ bit) for g in range(N_GRP)])  13.6 us
    all_to_all x1, starting transfers between devices, per_device(): lax.all_to_all(rows, 'freq', split_axis=0, concat_axis=0, axis_index_grou...  10.5 us
    ppermute x3, starting transfers between devices, gather_pivots(): lax.ppermute(value, 'grp', [(g, g ^ bit) for g in range(N_GRP)])  5.73 us
    pallas_call x1, Pallas kernels, spectra_rows(): pl.pallas_call(spectra_kernel, in_specs=[pl.BlockSpec(memory_space=pl.ANY...  4.75 us
    all_to_all x1, waiting for transfers between devices, per_device(): lax.all_to_all(rows, 'freq', split_axis=0, concat_axis=0, axis_index_grou...  3.49 us
    pallas_call x1, Pallas kernels, panel_rows(): pl.pallas_call(panel_kernel, in_specs=[pl.BlockSpec(memory_space=pltpu.VM...  2.15 us
    unnamed x10, local copies, waits for them, and re-layouts  1.91 us
    pallas_call x1, Pallas kernels, update_rows(): pl.pallas_call(update_kernel, in_specs=[pl.BlockSpec(memory_space=pltpu.V...  0.98 us
  transfers between devices with their start and end apart: 4, of which 4 were waited for; matrix products, arithmetic and copies ran while one was open for 0% of the time, Pallas kernels for 2%

profile of v6, /device:TPU:8, one launch (start us, length us, event | category | flops | bytes accessed | tf_op | source)
XLA Modules:
  0.0 43.4 jit_solution(13506995376926671201)
XLA Ops:
  0.0 0.0 copy-start.4
  0.0 0.0 copy-start.3
  0.0 4.8 %spectra.1 = bf16[128,2,16,128]{3,2,1,0:T(8,128)(2,1)} custom-call(bf16[8,2,2,128,512]{4,3,2,1,0:T(8,128)(2,1)} %bitcast.11, bf16[8,2,2,512,128]{4,3,2,1,0:T(8,128)(2,1)} %bitcast.12), custom_call_target="tpu_custom_call" | custom-call | tf_op jit(solution)/shard_map/spectra/pallas_call | solution.py:74
  4.8 0.0 copy-start.1
  4.8 0.0 copy-start.2
  4.8 10.5 %all-to-all-start = ((bf16[32,4,2,16,128]{4,3,2,1,0:T(8,128)(2,1)}), bf16[32,4,2,16,128]{4,3,2,1,0:T(8,128)(2,1)S(1)}, u32[]{:S(2)}, u32[]{:S(2)}) async-start(bf16[32,4,2,16,128]{4,3,2,1,0:T(8,128)(2,1)} %bitcast.10), calls=%async_computation | async-start | bytes 2097152 | tf_op jit(solution)/shard_map/all_to_all | solution.py:193
  15.3 0.0 copy-done.4
  15.3 0.1 broadcast_bitcast_fusion
  15.4 0.0 copy-done.3
  15.4 0.5 %collective-permute-start = (bf16[128,384]{1,0:T(8,128)(2,1)S(1)}, bf16[128,384]{1,0:T(8,128)(2,1)S(1)}, u32[]{:S(2)}, u32[]{:S(2)}) collective-permute-start(bf16[128,384]{1,0:T(8,128)(2,1)S(1)} %broadcast_select_fusion), channel_id=1, source_target_pairs={{0,32},{32,0},{64,96},{96,64},{128,160},{160,128},{192,224},{224,1... | collective-permute-start | bytes 294920 | tf_op jit(solution)/shard_map/ppermute | solution.py:186
  15.9 4.3 %collective-permute-done = bf16[128,384]{1,0:T(8,128)(2,1)S(1)} collective-permute-done((bf16[128,384]{1,0:T(8,128)(2,1)S(1)}, bf16[128,384]{1,0:T(8,128)(2,1)S(1)}, u32[]{:S(2)}, u32[]{:S(2)}) %collective-permute-start) | collective-permute-done | bytes 98336 | tf_op jit(solution)/shard_map/ppermute | solution.py:186
  20.3 2.4 %collective-permute-start.1 = (bf16[128,384]{1,0:T(8,128)(2,1)S(1)}, bf16[128,384]{1,0:T(8,128)(2,1)S(1)}, u32[]{:S(2)}, u32[]{:S(2)}) collective-permute-start(bf16[128,384]{1,0:T(8,128)(2,1)S(1)} %fusion), channel_id=1, source_target_pairs={{0,64},{32,96},{64,0},{96,32},{128,192},{160,224},{192,128},{224,1... | collective-permute-start | bytes 294920 | tf_op jit(solution)/shard_map/ppermute | solution.py:186
  22.7 3.8 %collective-permute-done.1 = bf16[128,384]{1,0:T(8,128)(2,1)S(1)} collective-permute-done((bf16[128,384]{1,0:T(8,128)(2,1)S(1)}, bf16[128,384]{1,0:T(8,128)(2,1)S(1)}, u32[]{:S(2)}, u32[]{:S(2)}) %collective-permute-start.1) | collective-permute-done | bytes 98336 | tf_op jit(solution)/shard_map/ppermute | solution.py:186
  26.5 2.8 %collective-permute-start.2 = (bf16[128,384]{1,0:T(8,128)(2,1)S(1)}, bf16[128,384]{1,0:T(8,128)(2,1)S(1)}, u32[]{:S(2)}, u32[]{:S(2)}) collective-permute-start(bf16[128,384]{1,0:T(8,128)(2,1)S(1)} %add.10), channel_id=1, source_target_pairs={{0,128},{32,160},{64,192},{96,224},{128,0},{160,32},{192,64},{224,... | collective-permute-start | bytes 294920 | tf_op jit(solution)/shard_map/ppermute | solution.py:186
  29.3 5.5 %collective-permute-done.2 = bf16[128,384]{1,0:T(8,128)(2,1)S(1)} collective-permute-done((bf16[128,384]{1,0:T(8,128)(2,1)S(1)}, bf16[128,384]{1,0:T(8,128)(2,1)S(1)}, u32[]{:S(2)}, u32[]{:S(2)}) %collective-permute-start.2) | collective-permute-done | bytes 98336 | tf_op jit(solution)/shard_map/ppermute | solution.py:186
  34.8 0.0 copy-start
  34.9 1.9 %copy-done = bf16[4096,384]{1,0:T(8,128)(2,1)S(1)} copy-done((bf16[4096,384]{1,0:T(8,128)(2,1)S(1)}, bf16[4096,384]{1,0:T(8,128)(2,1)}, u32[]{:S(2)}) %copy-start) | copy-done | bytes 3145752
  36.7 1.0 %update.1 = (bf16[4096,128]{1,0:T(8,128)(2,1)S(1)}, f8e5m2[4096,128]{1,0:T(32,128)(4,1)S(1)}) custom-call(bf16[4096,384]{1,0:T(8,128)(2,1)S(1)} %copy-done, bf16[128,384]{1,0:T(8,128)(2,1)S(1)} %add.11.pivots_ref), custom_call_target="tpu_custom_call" | custom-call | flops 402653184 | bytes 4718592 | tf_op jit(solution)/shard_map/update/pallas_call | solution.py:103
  37.7 3.5 %all-to-all-done.recv_ref = bf16[32,4,2,16,128]{4,3,2,1,0:T(8,128)(2,1)S(1)} async-done(((bf16[32,4,2,16,128]{4,3,2,1,0:T(8,128)(2,1)}), bf16[32,4,2,16,128]{4,3,2,1,0:T(8,128)(2,1)S(1)}, u32[]{:S(2)}, u32[]{:S(2)}) %all-to-all-start) | async-done | bytes 1048608 | tf_op jit(solution)/shard_map/all_to_all | solution.py:193
  41.2 0.0 copy-done.1
  41.2 0.0 copy-done.2
  41.2 2.1 %panel.1 = bf16[4,1024,128]{2,1,0:T(8,128)(2,1)} custom-call(bf16[768,512]{1,0:T(8,128)(2,1)S(1)} %copy-done.1, bf16[32,4,2,16,128]{4,3,2,1,0:T(8,128)(2,1)S(1)} %all-to-all-done.recv_ref, bf16[4,1024,128]{2,1,0:T(8,128)(2,1)S(1)} %bitcast.8, f8e5m2[4,1024,128]{2,1,0:T(32,128)(4,1)S(1)} %bitcast.9, bf16[128,128]{1,0:T(8,128)(2,1)S(1)} %copy-done.2), custom_call_target="tpu_custom_call" | custom-call | tf_op jit(solution)/shard_map/panel/pallas_call | solution.py:165
  (5 shorter events, 0.1 us)
Async XLA Ops:
  0.0 15.3 %copy-start.4 = (s32[3]{0:T(128)S(1)}, s32[3]{0:T(128)}, u32[]{:S(2)}) copy-start(s32[3]{0:T(128)} %param.11) | copy-start | bytes 40
  0.0 15.4 %copy-start.3 = (bf16[128,384]{1,0:T(8,128)(2,1)S(1)}, bf16[128,384]{1,0:T(8,128)(2,1)}, u32[]{:S(2)}) copy-start(bf16[128,384]{1,0:T(8,128)(2,1)} %param.10) | copy-start | bytes 294916
  4.8 36.5 %copy-start.1 = (bf16[768,512]{1,0:T(8,128)(2,1)S(1)}, bf16[768,512]{1,0:T(8,128)(2,1)}, u32[]{:S(2)}) copy-start(bf16[768,512]{1,0:T(8,128)(2,1)} %constant.10.clone.table_ref) | copy-start | bytes 2359300
  4.8 36.4 %copy-start.2 = (bf16[128,128]{1,0:T(8,128)(2,1)S(1)}, bf16[128,128]{1,0:T(8,128)(2,1)}, u32[]{:S(2)}) copy-start(bf16[128,128]{1,0:T(8,128)(2,1)} %inverse_hbm.1) | copy-start | bytes 98308
  4.8 36.4 %all-to-all-start = ((bf16[32,4,2,16,128]{4,3,2,1,0:T(8,128)(2,1)}), bf16[32,4,2,16,128]{4,3,2,1,0:T(8,128)(2,1)S(1)}, u32[]{:S(2)}, u32[]{:S(2)}) async-start(bf16[32,4,2,16,128]{4,3,2,1,0:T(8,128)(2,1)} %bitcast.10), calls=%async_computation | async-start | bytes 2097152 | tf_op jit(solution)/shard_map/all_to_all | solution.py:193
  15.4 4.9 %collective-permute-start = (bf16[128,384]{1,0:T(8,128)(2,1)S(1)}, bf16[128,384]{1,0:T(8,128)(2,1)S(1)}, u32[]{:S(2)}, u32[]{:S(2)}) collective-permute-start(bf16[128,384]{1,0:T(8,128)(2,1)S(1)} %broadcast_select_fusion), channel_id=1, source_target_pairs={{0,32},{32,0},{64,96},{96,64},{128,160},{160,128},{192,224},{224,1... | collective-permute-start | bytes 294920 | tf_op jit(solution)/shard_map/ppermute | solution.py:186
  20.3 6.2 %collective-permute-start.1 = (bf16[128,384]{1,0:T(8,128)(2,1)S(1)}, bf16[128,384]{1,0:T(8,128)(2,1)S(1)}, u32[]{:S(2)}, u32[]{:S(2)}) collective-permute-start(bf16[128,384]{1,0:T(8,128)(2,1)S(1)} %fusion), channel_id=1, source_target_pairs={{0,64},{32,96},{64,0},{96,32},{128,192},{160,224},{192,128},{224,1... | collective-permute-start | bytes 294920 | tf_op jit(solution)/shard_map/ppermute | solution.py:186
  26.5 8.3 %collective-permute-start.2 = (bf16[128,384]{1,0:T(8,128)(2,1)S(1)}, bf16[128,384]{1,0:T(8,128)(2,1)S(1)}, u32[]{:S(2)}, u32[]{:S(2)}) collective-permute-start(bf16[128,384]{1,0:T(8,128)(2,1)S(1)} %add.10), channel_id=1, source_target_pairs={{0,128},{32,160},{64,192},{96,224},{128,0},{160,32},{192,64},{224,... | collective-permute-start | bytes 294920 | tf_op jit(solution)/shard_map/ppermute | solution.py:186
  34.8 1.9 %copy-start = (bf16[4096,384]{1,0:T(8,128)(2,1)S(1)}, bf16[4096,384]{1,0:T(8,128)(2,1)}, u32[]{:S(2)}) copy-start(bf16[4096,384]{1,0:T(8,128)(2,1)} %lower_ref.1) | copy-start | bytes 9437188
